TPU v7x, 32 devices: a whole 2x2x4 slice. The times are simulated.
32 devices in a mesh: section: 4 (over x, core), fsdp: 8 (over z, y).
Axes of the slice: x: 2, y: 2, z: 4, core: 2. Of those that a mesh axis runs over, the one named last changes fastest.
Arguments:
- signals: bfloat16 [2048, 1536], P('fsdp', 'section'), may hold values from -6 to 6
- conv_weight: bfloat16 [768, 9, 1536], P('fsdp', None, 'section'), may hold values from -0.078125 to 0.078125
- buckets: int32 [2, 2], replicated, may hold values from 0 to 8, as said below
Outputs:
- results: bfloat16 [2048, 1536], P('fsdp', 'section')
- grad_weight: float32 [768, 9, 1536], P('fsdp', None, 'section')
Inputs may be any that keep to these rules, and one draw needn't show every extreme that they name: `buckets`: a bucket b means 16 + 2 b live pixels along that side, in the top left of each sample's grid; microbatch 0 has a height bucket of 5 or more; some entry is 8.
All inputs are finite; a program needn't handle non-finite values.
Results may differ from a plain program's by a relative error of at most 0.0054.
Values may be sent and summed in bfloat16 or wider, within the bound.
A program may use at most 128 MiB of HBM per device.

v0:
```python
import functools

import jax
import jax.numpy as jnp
from jax import lax
from jax.experimental import pallas as pl
from jax.experimental.pallas import tpu as pltpu
from jax.sharding import PartitionSpec as P

GROUPS = 32
SIDE = 32
MICRO = 2
ROWS_DEV = 8


eps = 1e-05


def from_partner(value, axis, stride):
    mask = 2**stride
    pairs = [(source, source ^ mask) for source in range(lax.axis_size(axis))]
    return lax.ppermute(value, axis, pairs)


def padded_2(cells, sides, width):
    for axis, dim in sides:
        count = lax.axis_size(axis)
        head = lax.slice_in_dim(cells, 0, width, axis=dim)
        tail = lax.slice_in_dim(cells, cells.shape[dim] - width, cells.shape[dim], axis=dim)
        cells = jnp.concatenate(
            [
                lax.ppermute(tail, axis, [(i, (i + 1) % count) for i in range(count)]),
                cells,
                lax.ppermute(head, axis, [((i + 1) % count, i) for i in range(count)]),
            ],
            axis=dim,
        )
    return cells


def silu_slope(value):
    sig = jax.nn.sigmoid(value)
    return sig * (1.0 + value * (1.0 - sig))


def section_swap(value, bit):
    return from_partner(value, "section", bit)


def general(signals, conv_weight, buckets):
    tok = signals.shape[0]
    half = signals.shape[1]
    width = 2 * half
    group_width = width // GROUPS
    local_groups = half // group_width
    section_index = lax.axis_index("section")
    upper_half = section_index % 2 == 1
    role_up = section_index >= 2
    fsdp_index = lax.axis_index("fsdp")
    pieces = SIDE // ROWS_DEV
    samples = lax.axis_size("fsdp") // pieces
    shifted = fsdp_index + 1
    sample_id = shifted // pieces % samples
    piece_id = shifted % pieces
    micro_id = sample_id // (samples // MICRO)
    picked_micro = jnp.arange(MICRO) == micro_id
    bucket_h = jnp.sum(jnp.where(picked_micro, buckets[:, 0], 0))
    bucket_w = jnp.sum(jnp.where(picked_micro, buckets[:, 1], 0))
    live_h = 16 + 2 * bucket_h
    live_w = 16 + 2 * bucket_w
    row_ids = piece_id * ROWS_DEV + jnp.arange(ROWS_DEV)
    col_ids = jnp.arange(SIDE)
    mask_grid = ((row_ids[:, None] < live_h) & (col_ids[None, :] < live_w)).astype(jnp.float32)
    mask_flat = mask_grid.reshape(tok, 1)
    group_count = (live_h * live_w).astype(jnp.float32) * group_width
    sample_hot = (jnp.arange(samples) == sample_id).astype(jnp.float32)[:, None]

    def with_rims(field):
        grid = field.reshape(ROWS_DEV, SIDE, field.shape[-1])
        padded = padded_2(grid, (("fsdp", 0),), 1)
        top = jnp.where(piece_id > 0, padded[:1], jnp.zeros_like(padded[:1]))
        bottom = jnp.where(piece_id < pieces - 1, padded[-1:], jnp.zeros_like(padded[-1:]))
        padded = jnp.concatenate([top, padded[1:-1], bottom], axis=0)
        return jnp.pad(padded, ((0, 0), (1, 1), (0, 0)))

    def group_totals(first, second):
        total_first, total_second = lax.psum(
            (sample_hot * first[None, :], sample_hot * second[None, :]), "fsdp"
        )
        return (
            jnp.sum(sample_hot * total_first, axis=0),
            jnp.sum(sample_hot * total_second, axis=0),
        )

    def normalize(values):
        grouped = values.reshape(tok, local_groups, group_width)
        masked = grouped * mask_flat[:, :, None]
        first = jnp.sum(masked, axis=(0, 2))
        second = jnp.sum(masked * masked, axis=(0, 2))
        total_first, total_second = group_totals(first, second)
        mean = total_first / group_count
        spread = total_second / group_count - mean * mean
        scale = lax.rsqrt(spread + eps)
        normed = (grouped - mean[None, :, None]) * scale[None, :, None]
        return (normed.reshape(tok, half), scale)

    def forward(inputs, weights):
        values = inputs.astype(jnp.float32)
        normed, scale = normalize(values)
        activated = (mask_flat * jax.nn.silu(normed)).astype(jnp.bfloat16)
        padded = with_rims(activated)
        partner = section_swap(padded, 0)
        lower = jnp.where(upper_half, partner, padded)
        upper = jnp.where(upper_half, padded, partner)
        full = jnp.concatenate([lower, upper], axis=-1)
        mixed = jnp.zeros((tok, half), jnp.float32)
        for tap in range(9):
            row_off, col_off = (tap // 3, tap % 3)
            slab = full[row_off : row_off + ROWS_DEV, col_off : col_off + SIDE].reshape(tok, width)
            mixed = mixed + jnp.dot(slab, weights[:, tap, :], preferred_element_type=jnp.float32)
        output = (values + mask_flat * mixed).astype(jnp.bfloat16)
        return (output, (normed, scale, full))

    def backward(grads, cache, weights):
        normed, scale, full = cache
        slope = (grads.astype(jnp.float32) * mask_flat).astype(jnp.bfloat16)
        padded = with_rims(slope)
        partial_value = jnp.zeros((tok, width), jnp.float32)
        for tap in range(9):
            row_off, col_off = (tap // 3, tap % 3)
            slab = padded[
                2 - row_off : 2 - row_off + ROWS_DEV, 2 - col_off : 2 - col_off + SIDE
            ].reshape(tok, half)
            partial_value = partial_value + lax.dot_general(
                slab,
                weights[:, tap, :],
                (((1,), (1,)), ((), ())),
                preferred_element_type=jnp.float32,
            )
        keep = jnp.where(upper_half, partial_value[:, half:], partial_value[:, :half])
        send = jnp.where(upper_half, partial_value[:, :half], partial_value[:, half:]).astype(
            jnp.bfloat16
        )
        arrived = section_swap(send, 0)
        kept = lax.optimization_barrier(keep.astype(jnp.bfloat16)).astype(jnp.float32)
        upstream = kept + arrived.astype(jnp.float32)
        gated = mask_flat * upstream * silu_slope(normed)
        grouped = gated.reshape(tok, local_groups, group_width)
        normed_grouped = normed.reshape(tok, local_groups, group_width)
        first = jnp.sum(grouped, axis=(0, 2))
        second = jnp.sum(grouped * normed_grouped, axis=(0, 2))
        total_first, total_second = group_totals(first, second)
        centred = (
            grouped
            - (total_first / group_count)[None, :, None]
            - normed_grouped * (total_second / group_count)[None, :, None]
        )
        through = mask_flat * (scale[None, :, None] * centred).reshape(tok, half)
        return (grads.astype(jnp.float32) + through, slope)

    weights = lax.all_gather(conv_weight, "fsdp", axis=0, tiled=True)
    start = (signals.astype(jnp.float32) * mask_flat).astype(jnp.bfloat16)
    first_out, first_cache = forward(start, weights)
    handed = section_swap(first_out, 1)
    second_out, second_cache = forward(handed, weights)
    back_weights = lax.all_gather(conv_weight, "fsdp", axis=0, tiled=True)
    up_grads, up_slope = backward(signals, second_cache, back_weights)
    returned = section_swap(up_grads.astype(jnp.bfloat16), 1)
    down_grads, down_slope = backward(returned, first_cache, back_weights)
    results = jnp.where(role_up, second_out, (mask_flat * down_grads).astype(jnp.bfloat16))
    chosen_full = jnp.where(role_up, second_cache[2], first_cache[2])
    chosen_slope = jnp.where(role_up, up_slope, down_slope)
    taps = []
    for tap in range(9):
        row_off, col_off = (tap // 3, tap % 3)
        slab = chosen_full[row_off : row_off + ROWS_DEV, col_off : col_off + SIDE].reshape(
            tok, width
        )
        taps.append(
            lax.dot_general(
                slab, chosen_slope, (((0,), (0,)), ((), ())), preferred_element_type=jnp.float32
            )
        )
    grad_weight = lax.psum_scatter(jnp.stack(taps, axis=1), "fsdp", scatter_dimension=0, tiled=True)
    return (results, grad_weight)


MESH = pl.DeviceIdType.MESH


def place():
    section = lax.axis_index("section")
    return section // 2, section % 2, lax.axis_index("fsdp")


def greet(peers):
    barrier = pltpu.get_barrier_semaphore()
    for peer in peers:
        pl.semaphore_signal(barrier, inc=1, device_id=peer, device_id_type=MESH)
    pl.semaphore_wait(barrier, len(peers))


def remote(src, dst, send, recv, peer):
    return pltpu.make_async_remote_copy(
        src_ref=src, dst_ref=dst, send_sem=send, recv_sem=recv, device_id=peer, device_id_type=MESH
    )


def landed(dst, sem):
    pltpu.make_async_copy(dst, dst, sem).wait()


def communicate(body, cid, args, outs, sems):
    return pl.pallas_call(
        body,
        out_shape=[jax.ShapeDtypeStruct(shape, jnp.bfloat16) for shape in outs],
        in_specs=[pl.BlockSpec(memory_space=pl.ANY)] * len(args),
        out_specs=[pl.BlockSpec(memory_space=pl.ANY)] * len(outs),
        scratch_shapes=[pltpu.SemaphoreType.DMA((count,)) for count in sems],
        compiler_params=pltpu.CompilerParams(collective_id=cid, has_side_effects=True),
    )(*args)


def across(f):
    return f + 1 - 2 * (f % 2)


def spread_kernel(n, rows_ref, slices_ref, cols_ref, full_ref, send_a, send_f, recv_a, send_g, recv_g):
    block, half, f = place()
    parts = n // 2
    piece = (f + 1) % n
    peers = []
    for d in range(1, 2 * n):
        other = (half * n + f + d) % (2 * n)
        peers.append((2 * block + other // n, other % n))
    greet(peers)
    for j0 in range(parts):
        j = (j0 + f) % parts
        to = parts * half + j

        @pl.when(to != f)
        def _():
            remote(
                slices_ref.at[j], cols_ref.at[piece], send_a.at[j0], recv_a.at[piece], (2 * block + half, to)
            ).start()

        @pl.when(to == f)
        def _():
            pltpu.make_async_copy(slices_ref.at[j], cols_ref.at[piece], recv_a.at[piece]).start()

    @pl.when(block == 1)
    def _():
        pltpu.make_async_copy(rows_ref, full_ref.at[piece], recv_g.at[piece]).start()
        for d in range(2, n, 2):
            remote(
                rows_ref, full_ref.at[piece], send_g.at[d], recv_g.at[piece], (2 + half, (f + d) % n)
            ).start()
        remote(rows_ref, full_ref.at[piece], send_g.at[0], recv_g.at[piece], (2 + half, across(f))).start()

    @pl.when(half == f // parts)
    def _():
        for p0 in range(n):
            p = (piece + p0) % n
            landed(cols_ref.at[p], recv_a.at[p])
            remote(
                cols_ref.at[p], cols_ref.at[p], send_f.at[p0], recv_a.at[p], (2 * block + 1 - half, f)
            ).start()
        for p0 in range(n):
            p = (piece + p0) % n
            pltpu.make_async_copy(cols_ref.at[p], cols_ref.at[p], send_f.at[p0]).wait()

    @pl.when(half != f // parts)
    def _():
        for p in range(n):
            landed(cols_ref.at[p], recv_a.at[p])

    for j0 in range(parts):
        j = (j0 + f) % parts

        @pl.when(parts * half + j != f)
        def _():
            pltpu.make_async_copy(slices_ref.at[j], slices_ref.at[j], send_a.at[j0]).wait()

    @pl.when(block == 1)
    def _():
        for d in range(2, n, 2):
            p = (piece + d) % n
            landed(full_ref.at[p], recv_g.at[p])
            remote(
                full_ref.at[p], full_ref.at[p], send_g.at[d + 1], recv_g.at[p], (2 + half, across(f))
            ).start()
        for d in range(0, n, 2):
            pltpu.make_async_copy(rows_ref, rows_ref, send_g.at[d]).wait()
        for d in range(2, n, 2):
            p = (piece + d) % n
            pltpu.make_async_copy(full_ref.at[p], full_ref.at[p], send_g.at[d + 1]).wait()
        landed(full_ref.at[piece], recv_g.at[piece])
        for d in range(0, n, 2):
            p = (across(f) + 1 + d) % n
            landed(full_ref.at[p], recv_g.at[p])


def reduce_kernel(n, role, mixed_ref, term_ref, parts_ref, other_ref, send, recv, send_t, recv_t):
    block, half, f = place()

    @pl.when(block == role)
    def _():
        greet([(2 * block + half, (f + d) % n) for d in range(1, n)])
        own = pltpu.make_async_copy(mixed_ref.at[(f + 1) % n], parts_ref.at[0], recv.at[0])
        own.start()
        copies = []
        for d in range(1, n):
            to = (f + d) % n
            copies.append(
                remote(
                    mixed_ref.at[(to + 1) % n],
                    parts_ref.at[d],
                    send.at[d],
                    recv.at[d],
                    (2 * block + half, to),
                )
            )
            copies[-1].start()
        own.wait()
        for copy in copies:
            copy.wait()

    @pl.when(block != role)
    def _():
        partner = (2 * block + 1 - half, f)
        greet([partner])
        copy = remote(term_ref, other_ref, send_t.at[0], recv_t.at[0], partner)
        copy.start()
        copy.wait()


def hand_kernel(n, slices_ref, rows_ref, cols_ref, own_ref, send, recv, send_f):
    block, half, f = place()
    parts = n // 2
    piece = (f + 1) % n

    @pl.when(block == 0)
    def _():
        greet([(2 + half, parts * half + j) for j in range(parts)] + [(2 + half, f)])
        copies = []
        for j0 in range(parts):
            j = (j0 + f) % parts
            copies.append(
                remote(
                    slices_ref.at[j],
                    cols_ref.at[piece],
                    send.at[j0],
                    recv.at[piece],
                    (2 + half, parts * half + j),
                )
            )
        copies.append(remote(rows_ref, own_ref, send.at[n], recv.at[n], (2 + half, f)))
        for copy in copies:
            copy.start()
        for copy in copies:
            copy.wait_send()

    @pl.when(jnp.logical_and(block == 1, half == f // parts))
    def _():
        greet([(half, i) for i in range(n)] + [(half, f), (3 - half, f)])
        for p0 in range(n):
            p = (piece + p0) % n
            landed(cols_ref.at[p], recv.at[p])
            remote(cols_ref.at[p], cols_ref.at[p], send_f.at[p0], recv.at[p], (3 - half, f)).start()
        for p0 in range(n):
            p = (piece + p0) % n
            pltpu.make_async_copy(cols_ref.at[p], cols_ref.at[p], send_f.at[p0]).wait()
        landed(own_ref, recv.at[n])

    @pl.when(jnp.logical_and(block == 1, half != f // parts))
    def _():
        greet([(half, f), (3 - half, f)])
        for p in range(n):
            landed(cols_ref.at[p], recv.at[p])
        landed(own_ref, recv.at[n])


def return_kernel(n, grads_ref, full_ref, cols_ref, send, recv, send_f):
    block, half, f = place()
    parts = n // 2

    @pl.when(block == 1)
    def _():
        line = [(f // parts, (f + d) % n) for d in range(0, n, 2)]
        greet(line + [(0, f), (1, f)])
        copies = []
        for i, peer in enumerate(line):
            copies.append(
                remote(
                    grads_ref.at[half],
                    full_ref.at[f % parts, half],
                    send.at[i],
                    recv.at[2 * (f % parts) + half],
                    peer,
                )
            )
        for core in range(2):
            copies.append(
                remote(
                    grads_ref.at[half],
                    cols_ref.at[half],
                    send.at[n + core],
                    recv.at[n + half],
                    (core, f),
                )
            )
        for copy in copies:
            copy.start()
        for copy in copies:
            copy.wait_send()

    @pl.when(block == 0)
    def _():
        near = [f % 2 + j for j in range(0, parts, 2)]
        far = [1 - f % 2 + j for j in range(0, parts, 2)]
        greet(
            [(2 + core, parts * half + j) for j in near for core in range(2)]
            + [(2, f), (3, f), (half, across(f))]
        )
        copies = []
        for i, j in enumerate(near):
            for core in range(2):
                landed(full_ref.at[j, core], recv.at[2 * j + core])
                copies.append(
                    remote(
                        full_ref.at[j, core],
                        full_ref.at[j, core],
                        send_f.at[2 * i + core],
                        recv.at[2 * j + core],
                        (half, across(f)),
                    )
                )
                copies[-1].start()
        for core in range(2):
            landed(cols_ref.at[core], recv.at[n + core])
        for copy in copies:
            copy.wait_send()
        for j in far:
            for core in range(2):
                landed(full_ref.at[j, core], recv.at[2 * j + core])


def taps_kernel(samples, active_ref, out_ref):
    area = SIDE * SIDE
    lanes = active_ref.shape[1]
    col = lax.broadcasted_iota(jnp.int32, (area, lanes), 0) % SIDE
    for s in range(samples):
        base = s * area
        here = active_ref[base : base + area, :].astype(jnp.float32)
        before = jnp.where(col > 0, pltpu.roll(here, 1, 0), 0.0).astype(jnp.bfloat16)
        after = jnp.where(col < SIDE - 1, pltpu.roll(here, area - 1, 0), 0.0).astype(jnp.bfloat16)
        edge = jnp.zeros((SIDE, lanes), jnp.bfloat16)
        for c, value in enumerate((before, here.astype(jnp.bfloat16), after)):
            up = slice(c * lanes, (c + 1) * lanes)
            mid = slice((3 + c) * lanes, (4 + c) * lanes)
            down = slice((6 + c) * lanes, (7 + c) * lanes)
            out_ref[base + SIDE : base + area, up] = value[: area - SIDE]
            out_ref[base : base + SIDE, up] = edge
            out_ref[base : base + area, mid] = value
            out_ref[base : base + area - SIDE, down] = value[SIDE:]
            out_ref[base + area - SIDE : base + area, down] = edge


def join_kernel(parts, slices_ref, out_ref):
    chan = slices_ref.shape[-1]
    for j in range(parts):
        out_ref[:, j * chan : (j + 1) * chan] = slices_ref[j]


def local(body, out, *args):
    return pl.pallas_call(
        body,
        out_shape=out,
        in_specs=[pl.BlockSpec(memory_space=pltpu.VMEM)] * len(args),
        out_specs=pl.BlockSpec(memory_space=pltpu.VMEM),
        compiler_params=pltpu.CompilerParams(vmem_limit_bytes=40 * 2**20),
    )(*args)


def collect_kernel(n, grads_ref, out_ref, send, recv):
    block, half, f = place()
    parts = n // 2

    @pl.when(block == 0)
    def _():
        greet(
            [((half * n + f + d) % (2 * n) // n, (half * n + f + d) % (2 * n) % n) for d in range(1, 2 * n)]
        )
        mine = f % parts
        for q0 in range(parts):
            piece = half * parts + (q0 + f) % parts
            to = (piece + n - 1) % n
            own = jnp.logical_and(to == f, half == f // parts)

            @pl.when(jnp.logical_not(own))
            def _():
                remote(
                    grads_ref.at[piece], out_ref.at[mine], send.at[q0], recv.at[mine], (f // parts, to)
                ).start()

            @pl.when(own)
            def _():
                pltpu.make_async_copy(grads_ref.at[piece], out_ref.at[mine], recv.at[mine]).start()

        for q0 in range(parts):
            piece = half * parts + (q0 + f) % parts
            own = jnp.logical_and((piece + n - 1) % n == f, half == f // parts)

            @pl.when(jnp.logical_not(own))
            def _():
                pltpu.make_async_copy(grads_ref.at[piece], grads_ref.at[piece], send.at[q0]).wait()

        for j in range(parts):
            landed(out_ref.at[j], recv.at[j])


def channel_split(signals, conv_weight, buckets):
    n = lax.axis_size("fsdp")
    tok, half = signals.shape
    chan = conv_weight.shape[0]
    parts = half // chan
    total = n * tok
    area = SIDE * SIDE
    samples = total // area
    group_width = 2 * half // GROUPS
    section = lax.axis_index("section")
    role_up = section >= 2
    f = lax.axis_index("fsdp")
    piece = (f + 1) % n
    bf16, f32 = jnp.bfloat16, jnp.float32

    live_h = jnp.repeat(16 + 2 * buckets[:, 0], samples // MICRO)
    live_w = jnp.repeat(16 + 2 * buckets[:, 1], samples // MICRO)
    cells = jnp.arange(SIDE)
    inside = (cells[None, :, None] < live_h[:, None, None]) & (cells[None, None, :] < live_w[:, None, None])
    mask = inside.astype(f32).reshape(samples, area, 1)
    mask_own = lax.dynamic_slice_in_dim(mask.reshape(total, 1), piece * tok, tok, axis=0)
    kcount = (live_h * live_w).astype(f32) * group_width

    def group_mean(value):
        columns = jnp.sum(value, axis=1)
        groups = jnp.sum(columns.reshape(samples, chan // group_width, group_width), axis=-1)
        return jnp.repeat(groups / kcount[:, None], group_width, axis=-1)[:, None, :]

    def normalize(values):
        masked = values * mask
        mean = group_mean(masked)
        spread = group_mean(masked * masked) - mean * mean
        scale = lax.rsqrt(spread + eps)
        normed = (values - mean) * scale
        return normed, scale, (mask * jax.nn.silu(normed)).astype(bf16)

    lanes = 128

    def taps_of(active):
        padded = jnp.pad(active.reshape(total, chan), ((0, 0), (0, lanes - chan)))
        return local(
            functools.partial(taps_kernel, samples),
            jax.ShapeDtypeStruct((total, 9 * lanes), bf16),
            padded,
        )

    def convolve(taps):
        weight = jnp.pad(conv_weight.transpose(1, 0, 2), ((0, 0), (0, lanes - chan), (0, 0)))
        return jnp.dot(taps, weight.reshape(9 * lanes, half), preferred_element_type=f32).reshape(n, tok, half)

    def convolve_back(slope):
        return (
            lax.conv_general_dilated(
                slope.reshape(samples, SIDE, SIDE, half),
                conv_weight[:, ::-1, :].transpose(1, 2, 0).reshape(3, 3, half, chan),
                (1, 1),
                "SAME",
                dimension_numbers=("NHWC", "HWIO", "NHWC"),
                preferred_element_type=f32,
            )
            .reshape(samples, area, chan)
            .astype(bf16)
        )

    def weight_slope(taps, slope):
        whole_taps = lax.dot_general(
            taps, slope.reshape(total, half), (((0,), (0,)), ((), ())), preferred_element_type=f32
        )
        return whole_taps.reshape(9, lanes, half)[:, :chan].transpose(1, 0, 2)

    def input_slope(term, other, normed, scale, grads):
        upstream = term.astype(f32) + other.astype(f32)
        gated = mask * upstream * silu_slope(normed)
        first = group_mean(gated)
        second = group_mean(gated * normed)
        return grads.astype(f32) + mask * (scale * (gated - first - normed * second))

    def sliced(rows):
        return rows.reshape(tok, parts, chan).transpose(1, 0, 2)

    whole = (samples, area, chan)
    cols, full = communicate(
        functools.partial(spread_kernel, n),
        0,
        (signals, sliced(signals)),
        [(n, tok, chan), (n, tok, half)],
        (parts, n, n, n, n),
    )
    cols = cols.reshape(whole)

    values = (cols.astype(f32) * mask).astype(bf16).astype(f32)
    normed_down, scale_down, active_down = normalize(values)
    taps_down = taps_of(active_down)

    def first_down():
        return convolve(taps_down).astype(bf16), jnp.zeros(whole, bf16)

    def first_up():
        slope = (full.reshape(samples, area, half).astype(f32) * mask).astype(bf16)
        return jnp.zeros((n, tok, half), bf16), convolve_back(slope)

    mixed, term = lax.cond(role_up, first_up, first_down)
    partial_rows, other = communicate(
        functools.partial(reduce_kernel, n, 0),
        1,
        (mixed, term),
        [(n, tok, half), whole],
        (n, n, 1, 1),
    )

    def block_rows(rows, pieces):
        return (rows + mask_own * jnp.sum(pieces.astype(f32), axis=0)).astype(bf16)

    start_rows = (signals.astype(f32) * mask_own).astype(bf16).astype(f32)
    handed = block_rows(start_rows, partial_rows)
    skip_cols, skip_rows = communicate(
        functools.partial(hand_kernel, n),
        2,
        (sliced(handed), handed),
        [(n, tok, chan), (tok, half)],
        (n + 1, n + 1, n),
    )

    def second_up():
        normed, scale, active = normalize(skip_cols.reshape(whole).astype(f32))
        slope = mask * input_slope(term, other, normed, scale, cols)
        return slope.astype(bf16), active

    def second_down():
        return jnp.zeros(whole, bf16), jnp.zeros(whole, bf16)

    grads, active_up = lax.cond(role_up, second_up, second_down)
    back, back_cols = communicate(
        functools.partial(return_kernel, n),
        3,
        (grads.reshape(2, total // 2, chan),),
        [(parts, 2, total // 2, chan), (2, total // 2, chan)],
        (n + 2, n + 2, n),
    )

    def third_up():
        slope = (full.reshape(samples, area, half).astype(f32) * mask).astype(bf16)
        taps_up = taps_of(active_up)
        return convolve(taps_up).astype(bf16), jnp.zeros(whole, bf16), weight_slope(taps_up, slope)

    def third_down():
        slope = local(
            functools.partial(join_kernel, parts),
            jax.ShapeDtypeStruct((total, half), bf16),
            back.reshape(parts, total, chan),
        )
        return jnp.zeros((n, tok, half), bf16), convolve_back(slope), weight_slope(taps_down, slope)

    mixed, term, grad_weight = lax.cond(role_up, third_up, third_down)
    partial_rows, other = communicate(
        functools.partial(reduce_kernel, n, 1),
        4,
        (mixed, term),
        [(n, tok, half), whole],
        (n, n, 1, 1),
    )

    def last_down():
        slope = input_slope(term, other, normed_down, scale_down, back_cols.reshape(whole))
        return (mask * slope).astype(bf16)

    def last_up():
        return jnp.zeros(whole, bf16)

    grads = lax.cond(role_up, last_up, last_down)
    (pieces,) = communicate(
        functools.partial(collect_kernel, n),
        5,
        (grads.reshape(n, tok, chan),),
        [(parts, tok, chan)],
        (parts, parts),
    )
    down_rows = pieces.transpose(1, 0, 2).reshape(tok, half)
    results = jnp.where(role_up, block_rows(skip_rows.astype(f32), partial_rows), down_rows)
    return results, grad_weight


def per_device(signals, conv_weight, buckets):
    n = lax.axis_size("fsdp")
    chan = conv_weight.shape[0]
    half = signals.shape[1]
    fits = (
        lax.axis_size("section") == 4
        and n % 4 == 0
        and chan <= 128
        and chan % (2 * half // GROUPS) == 0
        and half == chan * (n // 2)
        and n * signals.shape[0] == MICRO * SIDE * SIDE
    )
    return (channel_split if fits else general)(signals, conv_weight, buckets)


def solution(mesh):
    return jax.shard_map(
        per_device,
        mesh=mesh,
        in_specs=(P("fsdp", "section"), P("fsdp", None, "section"), P()),
        out_specs=(P("fsdp", "section"), P("fsdp", None, "section")),
        check_vma=False,
    )
```

profile of v0, /device:TPU:14, one launch (start us, length us, event | category | flops | bytes accessed | tf_op | source)
XLA Modules:
  0.0 186.5 jit_solution(5886025965185614605)
XLA Ops:
  0.6 1.0 fusion.36
  1.8 1.1 copy.56
  2.9 0.8 copy.57
  3.8 38.7 %shard_map.50 = (bf16[8,256,96]{2,1,0:T(8,128)(2,1)S(1)}, bf16[8,256,384]{2,1,0:T(8,128)(2,1)S(1)}) custom-call(bf16[256,384]{1,0:T(8,128)(2,1)} %rows_ref.1, bf16[4,256,96]{2,1,0:T(8,128)(2,1)} %bitcast.150), custom_call_target="tpu_custom_call" | custom-call | tf_op jit(solution)/shard_map/pallas_call | solution.py:214
  42.5 0.4 fusion.33
  42.8 0.1 reshape.332
  42.9 0.1 reduce_sum.193
  43.0 0.1 reshape.333
  43.1 0.1 reduce_sum.197
  43.2 0.9 multiply_reduce_fusion.5
  44.3 0.1 sub.81
  44.5 0.1 broadcast_in_dim_reshape.4
  44.6 0.5 multiply_convert_fusion.5
  45.1 0.1 pad.14.active_ref
  45.2 2.8 %shard_map.51 = bf16[2048,1152]{1,0:T(8,128)(2,1)} custom-call(bf16[2048,128]{1,0:T(8,128)(2,1)S(1)} %pad.14.active_ref), custom_call_target="tpu_custom_call" | custom-call | tf_op jit(solution)/shard_map/pallas_call | solution.py:476
  48.2 10.6 %conditional.4 = (bf16[8,256,384]{2,1,0:T(8,128)(2,1)S(1)}, bf16[2,1024,96]{2,1,0:T(8,128)(2,1)S(1)}) conditional(s32[]{:T(128)} %convert_element_type.211, (bf16[96,9,384]{2,0,1:T(8,128)(2,1)S(1)}, bf16[2048,1152]{1,0:T(8,128)(2,1)}) %tuple.80, (bf16[8,256,384]{2,1,0:T(8,128)(2,1)S(1)}, f32[2,1024,1]{1,2,0:T(1,128)S(1)}, ...), branch_computations={%region_6.7_spmd, %region_7.8_spmd} | conditional | flops 1812725760 | bytes 26018240 | solution.py:623
  48.4 0.3 fusion.7
  48.8 0.6 copy.65
  49.4 0.2 pad.15.clone
  49.5 0.1 slice.19
  49.7 1.8 fusion.3
  51.6 6.5 %fusion.11 = bf16[32,16,5,96]{3,1,2,0:T(8,128)(2,1)S(1)} fusion(bf16[3,3,384,96]{2,3,1,0:T(8,128)(2,1)S(1)} %bitcast.157, bf16[32,2,8,7,384]{4,0,3,2,1:T(8,128)(2,1)} %fusion.3, pred[16,5]{0,1:T(8,128)(4,1)S(1)} %copy-done.8), kind=kOutput, calls=%fused_computation.12 | convolution fusion | flops 1663795200 | bytes 3907664 | tf_op jit(solution)/shard_map/cond/branch_1_fun/conv_general_dilated | solution.py:574
  58.1 0.2 copy.49
  58.4 0.2 copy.50
  58.6 0.1 broadcast.136
  58.7 2.3 %shard_map.52 = (bf16[8,256,384]{2,1,0:T(8,128)(2,1)}, bf16[2,1024,96]{2,1,0:T(8,128)(2,1)}) custom-call(bf16[8,256,384]{2,1,0:T(8,128)(2,1)S(1)} %get-tuple-element.120.mixed_ref, bf16[2,1024,96]{2,1,0:T(8,128)(2,1)S(1)} %get-tuple-element.121.term_ref), custom_call_target="tpu_custom_call" | custom-call | tf_op jit(solution)/shard_map/pallas_call | solution.py:214
  61.0 1.7 convert_reduce_fusion.1
  62.8 0.1 add_convert_fusion.1.rows_ref
  62.9 0.1 copy.59
  63.1 0.8 copy.60
  63.9 17.7 %shard_map.53 = (bf16[8,256,96]{2,1,0:T(8,128)(2,1)S(1)}, bf16[256,384]{1,0:T(8,128)(2,1)}) custom-call(bf16[4,256,96]{2,1,0:T(8,128)(2,1)} %bitcast.149, bf16[256,384]{1,0:T(8,128)(2,1)} %copy-done.6), custom_call_target="tpu_custom_call" | custom-call | tf_op jit(solution)/shard_map/pallas_call | solution.py:214
  81.6 7.7 %conditional.5 = (bf16[2,1024,96]{2,1,0:T(8,128)(2,1)}, bf16[2,1024,96]{2,1,0:T(8,128)(2,1)}) conditional(s32[]{:T(128)} %convert_element_type.211, () %tuple.40, (f32[2,1024,1]{1,2,0:T(1,128)S(1)}, bf16[2,1024,96]{2,1,0:T(8,128)(2,1)S(1)}, bf16[8,256,96]{2,1,0:T(8,128)(2,1)S(1)}, f32[2]{0:T(128)S(1)}, bf16[2,1024,96]{2,1,0:T(8,128)(2,1)S(1)}, ...), branch_computations={%region_9.10_spmd, %region_10.21_spmd} | conditional | flops 7864896 | bytes 6799676 | solution.py:653
  81.7 0.4 multiply_reduce_fusion.2
  82.1 0.1 reshape.310
  82.1 0.1 reduce_sum.115
  82.3 0.1 reshape.312
  82.3 0.1 reduce_sum.148
  82.6 0.1 reshape.313
  82.7 0.1 reshape.311
  82.8 0.1 convert_element_type.157
  82.9 2.7 %fusion.38 = (f32[2,96]{1,0:T(2,128)S(1)}, f32[2,96]{1,0:T(2,128)S(1)}, f32[2,1024,96]{2,1,0:T(8,128)}) fusion(f32[2,96]{1,0:T(2,128)S(1)} %add_rsqrt_fusion.1, f32[2,96]{1,0:T(2,128)S(1)} %reshape.313, bf16[2,1024,96]{2,1,0:T(8,128)(2,1)} %get-tuple-element.81, bf16[2,1024,96]{2,1,0:T(8,128)(2,1)S(1)} %get-tuple-element.80, f32[2,1024]{1,0:T(2,128)S(1)} %bitcast.159, ...), kind=kLoop, calls=%fused_computation.84 | loop fusion | flops 3341952 | bytes 2370560 | tf_op jit(solution)/shard_map/cond/branch_1_fun/reduce_sum | solution.py:546
  85.7 0.1 reduce_sum.150
  85.9 0.1 reduce_sum.155
  86.2 0.1 mul.241
  86.3 0.1 sub.64
  86.4 2.9 %multiply_convert_fusion.1 = (bf16[2,1024,96]{2,1,0:T(8,128)(2,1)}, bf16[2,1024,96]{2,1,0:T(8,128)(2,1)}) fusion(f32[2,96]{1,0:T(2,128)S(1)} %reshape.313, f32[2,96]{1,0:T(2,128)S(1)} %add_rsqrt_fusion.1, f32[2,1024]{1,0:T(2,128)S(1)} %bitcast.160, f32[2,96]{1,0:T(2,128)S(1)} %mul.241, f32[2,1024,96]{2,1,0:T(8,128)} %get-tuple-element.181, ...), kind=kLoop, calls=%fused_computation.36 | loop fusion | flops 3342336 | bytes 2763776 | tf_op jit(solution)/shard_map/cond/branch_1_fun/convert_element_type | solution.py:556
  89.3 32.9 %shard_map.54 = (bf16[4,2,1024,96]{3,2,1,0:T(8,128)(2,1)}, bf16[2,1024,96]{2,1,0:T(8,128)(2,1)}) custom-call(bf16[2,1024,96]{2,1,0:T(8,128)(2,1)} %get-tuple-element.126.grads_ref), custom_call_target="tpu_custom_call" | custom-call | tf_op jit(solution)/shard_map/pallas_call | solution.py:214
  122.2 21.0 %conditional.6 = (bf16[8,256,384]{2,1,0:T(8,128)(2,1)}, bf16[2,1024,96]{2,1,0:T(8,128)(2,1)S(1)}, f32[96,9,384]{2,0,1:T(8,128)}) conditional(s32[]{:T(128)} %convert_element_type.211, (bf16[4,2,1024,96]{3,2,1,0:T(8,128)(2,1)}, bf16[96,9,384]{2,0,1:T(8,128)(2,1)S(1)}, bf16[2048,1152]{1,0:T(8,128)(2,1)}) %tuple.82, (bf16[2,1024,96]{2,1,0:T(8,128)(2,1)}, ...), branch_computations={%region_21.22_spmd, %region_22.23_spmd} | conditional | flops 3483992064 | bytes 68419720 | solution.py:675
  122.7 1.1 pad.11.active_ref
  123.8 0.7 branch_1_fun.1
  124.5 2.2 %copy-done = bf16[2048,1152]{1,0:T(8,128)(2,1)} copy-done((bf16[2048,1152]{1,0:T(8,128)(2,1)}, bf16[2048,1152]{1,0:T(8,128)(2,1)S(1)}, u32[]{:S(2)}) %copy-start) | copy-done | bytes 4718616 | tf_op jit(solution)/shard_map/cond
  126.7 6.8 %copy.55 = bf16[1152,2048]{1,0:T(8,128)(2,1)} copy(bf16[1152,2048]{0,1:T(8,128)(2,1)} %bitcast.122) | data formatting | bytes 9437184 | tf_op jit(solution)/shard_map/cond/branch_1_fun/dot_general | solution.py:587
  133.5 0.3 multiply_convert_fusion.3
  133.9 5.2 %fusion.29 = f32[96,9,384]{2,0,1:T(8,128)} fusion(bf16[2048,384,1]{1,0,2:T(8,128)(2,1)S(1)} %bitcast.147, bf16[9,128,2048]{2,1,0:T(8,128)(2,1)} %bitcast.141), kind=kOutput, calls=%fused_computation.53 | convolution fusion | flops 1358954496 | bytes 6438912 | tf_op jit(solution)/shard_map/cond/branch_1_fun/dot_general | solution.py:587
  139.1 0.1 pad.12
  139.3 3.8 %convolution_convert_fusion.1 = bf16[8,256,384]{2,1,0:T(8,128)(2,1)} fusion(bf16[8,256,1152]{2,1,0:T(8,128)(2,1)S(1)} %bitcast.125, bf16[1152,384,1]{1,0,2:T(8,128)(2,1)S(1)} %bitcast.152), kind=kOutput, calls=%fused_computation.52 | convolution fusion | flops 1812725760 | bytes 7176192 | tf_op jit(solution)/shard_map/cond/branch_1_fun/dot_general | solution.py:570
  143.2 38.9 %shard_map.55 = (bf16[8,256,384]{2,1,0:T(8,128)(2,1)}, bf16[2,1024,96]{2,1,0:T(8,128)(2,1)}) custom-call(bf16[8,256,384]{2,1,0:T(8,128)(2,1)} %get-tuple-element.129.mixed_ref, bf16[2,1024,96]{2,1,0:T(8,128)(2,1)S(1)} %get-tuple-element.130.term_ref), custom_call_target="tpu_custom_call" | custom-call | tf_op jit(solution)/shard_map/pallas_call | solution.py:214
  182.2 0.3 fusion.34
  182.6 0.1 conditional.7
  182.7 0.1 shard_map.56
  182.8 1.1 copy.62
  183.9 0.2 copy.63
  184.0 1.7 convert_reduce_fusion
  185.7 0.8 fusion.35
  (58 shorter events, 2.0 us)
Async XLA Ops:
  42.4 5.7 %copy-start.2 = (bf16[8,256,384]{2,1,0:T(8,128)(2,1)}, bf16[8,256,384]{2,1,0:T(8,128)(2,1)S(1)}, u32[]{:S(2)}) copy-start(bf16[8,256,384]{2,1,0:T(8,128)(2,1)S(1)} %get-tuple-element.119) | copy-start | bytes 4718596
  45.2 2.9 %copy-start.1 = (bf16[96,9,384]{2,0,1:T(8,128)(2,1)S(1)}, bf16[96,9,384]{2,0,1:T(8,128)(2,1)}, u32[]{:S(2)}) copy-start(bf16[96,9,384]{2,0,1:T(8,128)(2,1)} %param.12) | copy-start | bytes 1990660
  49.7 1.9 %copy-start.8 = (pred[16,5]{0,1:T(8,128)(4,1)S(1)}, pred[16,5]{0,1:T(8,128)(4,1)}, u32[]{:S(2)}) copy-start(pred[16,5]{0,1:T(8,128)(4,1)} %constant.89) | copy-start | bytes 244 | tf_op jit(solution)/shard_map/cond
  58.7 4.1 %copy-start.5 = (bf16[256,384]{1,0:T(8,128)(2,1)S(1)}, bf16[256,384]{1,0:T(8,128)(2,1)}, u32[]{:S(2)}) copy-start(bf16[256,384]{1,0:T(8,128)(2,1)} %rows_ref.1) | copy-start | bytes 589828
  62.9 1.0 copy-start.6
  124.5 2.2 %copy-start = (bf16[2048,1152]{1,0:T(8,128)(2,1)}, bf16[2048,1152]{1,0:T(8,128)(2,1)S(1)}, u32[]{:S(2)}) copy-start(bf16[2048,1152]{1,0:T(8,128)(2,1)S(1)} %branch_1_fun.1) | copy-start | bytes 14155780 | tf_op jit(solution)/shard_map/cond
  126.7 6.9 %copy-start.3 = (bf16[8,256,384]{2,1,0:T(8,128)(2,1)S(1)}, bf16[8,256,384]{2,1,0:T(8,128)(2,1)}, u32[]{:S(2)}) copy-start(bf16[8,256,384]{2,1,0:T(8,128)(2,1)} %get-tuple-element.87) | copy-start | bytes 4718596 | tf_op jit(solution)/shard_map/cond
  133.5 5.7 %slice-start = ((s8[4718592]{0:T(1024)(128)(4,1)}), s8[4194304]{0:T(1024)(128)(4,1)S(1)}, s32[]{:S(2)}) async-start(s8[4718592]{0:T(1024)(128)(4,1)} %bitcast.123), calls=%async_computation | async-start | bytes 8388608 | tf_op jit(solution)/shard_map/cond
  133.9 5.4 %slice-start.1 = ((s8[4718592]{0:T(1024)(128)(4,1)}), s8[524288]{0:T(1024)(128)(4,1)S(1)}, s32[]{:S(2)}) async-start(s8[4718592]{0:T(1024)(128)(4,1)} %bitcast.123), calls=%async_computation.1 | async-start | bytes 1048576 | tf_op jit(solution)/shard_map/cond
  182.7 3.0 %copy-start.7 = (bf16[256,384]{1,0:T(8,128)(2,1)S(1)}, bf16[256,384]{1,0:T(8,128)(2,1)}, u32[]{:S(2)}) copy-start(bf16[256,384]{1,0:T(8,128)(2,1)} %get-tuple-element.123) | copy-start | bytes 589828
where the time goes:
time: 187 us
  Pallas kernels  134 us (72%)
  local copies, waits for them, and re-layouts  18.1 us (10%)
  other arithmetic  17 us (9%)
  matrix products  15.6 us (8%)
    pallas_call x6, Pallas kernels, communicate(): pl.pallas_call(body, out_shape=[jax.ShapeDtypeStruct(shape, jnp.bfloat16)...  130 us
    dot_general x1, local copies, waits for them, and re-layouts, weight_slope(): lax.dot_general(taps, slope.reshape(total, half), (((0,), (0,)), ((), ())...  6.8 us
    conv_general_dilated x1, matrix products, convolve_back(): lax.conv_general_dilated(slope.reshape(samples, SIDE, SIDE, half), conv_w...  6.54 us
    dot_general x1, matrix products, weight_slope(): lax.dot_general(taps, slope.reshape(total, half), (((0,), (0,)), ((), ())...  5.23 us
    dot_general x1, matrix products, convolve(): jnp.dot(taps, weight.reshape(9 * lanes, half), preferred_element_type=f32)  3.83 us

commit v1 on v0

--- a/solution.py
+++ b/solution.py
@@ -210,14 +210,18 @@
     pltpu.make_async_copy(dst, dst, sem).wait()
 
 
-def communicate(body, cid, args, outs, sems):
+def communicate(body, cid, args, outs, sems, scratch=(), fast=()):
+    spaces = [pltpu.VMEM if i in fast else pl.ANY for i in range(len(args) + len(outs))]
+    specs = [pl.BlockSpec(memory_space=space) for space in spaces]
     return pl.pallas_call(
         body,
-        out_shape=[jax.ShapeDtypeStruct(shape, jnp.bfloat16) for shape in outs],
-        in_specs=[pl.BlockSpec(memory_space=pl.ANY)] * len(args),
-        out_specs=[pl.BlockSpec(memory_space=pl.ANY)] * len(outs),
-        scratch_shapes=[pltpu.SemaphoreType.DMA((count,)) for count in sems],
-        compiler_params=pltpu.CompilerParams(collective_id=cid, has_side_effects=True),
+        out_shape=[jax.ShapeDtypeStruct(shape, dtype) for shape, dtype in outs],
+        in_specs=specs[: len(args)],
+        out_specs=specs[len(args) :],
+        scratch_shapes=list(scratch) + [pltpu.SemaphoreType.DMA((count,)) for count in sems],
+        compiler_params=pltpu.CompilerParams(
+            collective_id=cid, has_side_effects=True, vmem_limit_bytes=40 * 2**20
+        ),
     )(*args)
 
 
@@ -257,6 +261,15 @@
             ).start()
         remote(rows_ref, full_ref.at[piece], send_g.at[0], recv_g.at[piece], (2 + half, across(f))).start()
 
+    @pl.when(block == 1)
+    def _():
+        for d in range(2, n, 2):
+            p = (piece + d) % n
+            landed(full_ref.at[p], recv_g.at[p])
+            remote(
+                full_ref.at[p], full_ref.at[p], send_g.at[d + 1], recv_g.at[p], (2 + half, across(f))
+            ).start()
+
     @pl.when(half == f // parts)
     def _():
         for p0 in range(n):
@@ -274,21 +287,8 @@
         for p in range(n):
             landed(cols_ref.at[p], recv_a.at[p])
 
-    for j0 in range(parts):
-        j = (j0 + f) % parts
-
-        @pl.when(parts * half + j != f)
-        def _():
-            pltpu.make_async_copy(slices_ref.at[j], slices_ref.at[j], send_a.at[j0]).wait()
-
     @pl.when(block == 1)
     def _():
-        for d in range(2, n, 2):
-            p = (piece + d) % n
-            landed(full_ref.at[p], recv_g.at[p])
-            remote(
-                full_ref.at[p], full_ref.at[p], send_g.at[d + 1], recv_g.at[p], (2 + half, across(f))
-            ).start()
         for d in range(0, n, 2):
             pltpu.make_async_copy(rows_ref, rows_ref, send_g.at[d]).wait()
         for d in range(2, n, 2):
@@ -299,31 +299,60 @@
             p = (across(f) + 1 + d) % n
             landed(full_ref.at[p], recv_g.at[p])
 
-
-def reduce_kernel(n, role, mixed_ref, term_ref, parts_ref, other_ref, send, recv, send_t, recv_t):
+    for j0 in range(parts):
+        j = (j0 + f) % parts
+
+        @pl.when(parts * half + j != f)
+        def _():
+            pltpu.make_async_copy(slices_ref.at[j], slices_ref.at[j], send_a.at[j0]).wait()
+
+
+def reduce_kernel(
+    n, role, mixed_ref, term_ref, sum_ref, other_ref, near, pair, far, send, recv, send_z, recv_z, send_t, recv_t
+):
     block, half, f = place()
 
     @pl.when(block == role)
     def _():
-        greet([(2 * block + half, (f + d) % n) for d in range(1, n)])
-        own = pltpu.make_async_copy(mixed_ref.at[(f + 1) % n], parts_ref.at[0], recv.at[0])
-        own.start()
+        section = 2 * block + half
+        greet([(section, across(f))] + [(section, (f + d) % n) for d in range(2, n, 2)])
+        order = sorted(range(0, n, 2), key=lambda d: -min(d, n - d))
         copies = []
-        for d in range(1, n):
-            to = (f + d) % n
+        for d in order:
+            to = (across(f) + d) % n
             copies.append(
                 remote(
                     mixed_ref.at[(to + 1) % n],
-                    parts_ref.at[d],
-                    send.at[d],
-                    recv.at[d],
-                    (2 * block + half, to),
+                    near.at[d // 2],
+                    send.at[d // 2],
+                    recv.at[d // 2],
+                    (section, across(f)),
                 )
             )
             copies[-1].start()
-        own.wait()
-        for copy in copies:
-            copy.wait()
+        onward = []
+        for d, copy in zip(order, copies):
+            copy.wait_recv()
+            both = mixed_ref[(f + d + 1) % n].astype(jnp.float32) + near[d // 2].astype(jnp.float32)
+            if d:
+                pair[d // 2] = both.astype(jnp.bfloat16)
+                onward.append(
+                    remote(
+                        pair.at[d // 2],
+                        far.at[d // 2],
+                        send_z.at[d // 2],
+                        recv_z.at[d // 2],
+                        (section, (f + d) % n),
+                    )
+                )
+                onward[-1].start()
+            else:
+                sum_ref[...] = both
+        for d, copy in zip(order, onward):
+            copy.wait_recv()
+            sum_ref[...] += far[d // 2].astype(jnp.float32)
+        for copy in copies + onward:
+            copy.wait_send()
 
     @pl.when(block != role)
     def _():
@@ -380,31 +409,28 @@
         landed(own_ref, recv.at[n])
 
 
-def return_kernel(n, grads_ref, full_ref, cols_ref, send, recv, send_f):
+def return_kernel(n, grads_ref, full_ref, cols_ref, send, recv, send_z, send_f):
     block, half, f = place()
     parts = n // 2
 
     @pl.when(block == 1)
     def _():
-        line = [(f // parts, (f + d) % n) for d in range(0, n, 2)]
-        greet(line + [(0, f), (1, f)])
-        copies = []
-        for i, peer in enumerate(line):
-            copies.append(
-                remote(
-                    grads_ref.at[half],
-                    full_ref.at[f % parts, half],
-                    send.at[i],
-                    recv.at[2 * (f % parts) + half],
-                    peer,
-                )
+        greet([(0, f), (1, f)])
+        copies = [
+            remote(
+                grads_ref.at[half],
+                full_ref.at[half, f % parts],
+                send.at[0],
+                recv.at[2 * (f % parts) + half],
+                (f // parts, f),
             )
+        ]
         for core in range(2):
             copies.append(
                 remote(
                     grads_ref.at[half],
                     cols_ref.at[half],
-                    send.at[n + core],
+                    send.at[1 + core],
                     recv.at[n + half],
                     (core, f),
                 )
@@ -416,33 +442,44 @@
 
     @pl.when(block == 0)
     def _():
-        near = [f % 2 + j for j in range(0, parts, 2)]
-        far = [1 - f % 2 + j for j in range(0, parts, 2)]
-        greet(
-            [(2 + core, parts * half + j) for j in near for core in range(2)]
-            + [(2, f), (3, f), (half, across(f))]
-        )
+        line = [(half, (f + d) % n) for d in sorted(range(2, n, 2), key=lambda d: -min(d, n - d))]
+        greet([(2, f), (3, f), (half, across(f))] + line)
+        steps = parts // 2
+        near = [f % 2 + 2 * ((i + f // 2) % steps) for i in range(steps)]
+        far = [1 - f % 2 + 2 * ((i + f // 2) % steps) for i in range(steps)]
         copies = []
         for i, j in enumerate(near):
             for core in range(2):
-                landed(full_ref.at[j, core], recv.at[2 * j + core])
+                slot = full_ref.at[core, j]
+                landed(slot, recv.at[2 * j + core])
+                if i == 0:
+
+                    @pl.when(parts * half + j == f)
+                    def _():
+                        for q, peer in enumerate(line):
+                            remote(
+                                slot, slot, send_z.at[2 * q + core], recv.at[2 * j + core], peer
+                            ).start()
+
                 copies.append(
-                    remote(
-                        full_ref.at[j, core],
-                        full_ref.at[j, core],
-                        send_f.at[2 * i + core],
-                        recv.at[2 * j + core],
-                        (half, across(f)),
-                    )
+                    remote(slot, slot, send_f.at[2 * i + core], recv.at[2 * j + core], (half, across(f)))
                 )
                 copies[-1].start()
         for core in range(2):
             landed(cols_ref.at[core], recv.at[n + core])
         for copy in copies:
             copy.wait_send()
+
+        @pl.when(parts * half + near[0] == f)
+        def _():
+            for q in range(len(line)):
+                for core in range(2):
+                    slot = full_ref.at[core, near[0]]
+                    pltpu.make_async_copy(slot, slot, send_z.at[2 * q + core]).wait()
+
         for j in far:
             for core in range(2):
-                landed(full_ref.at[j, core], recv.at[2 * j + core])
+                landed(full_ref.at[core, j], recv.at[2 * j + core])
 
 
 def taps_kernel(samples, active_ref, out_ref):
@@ -466,12 +503,6 @@
             out_ref[base + area - SIDE : base + area, down] = edge
 
 
-def join_kernel(parts, slices_ref, out_ref):
-    chan = slices_ref.shape[-1]
-    for j in range(parts):
-        out_ref[:, j * chan : (j + 1) * chan] = slices_ref[j]
-
-
 def local(body, out, *args):
     return pl.pallas_call(
         body,
@@ -604,7 +635,7 @@
         functools.partial(spread_kernel, n),
         0,
         (signals, sliced(signals)),
-        [(n, tok, chan), (n, tok, half)],
+        [((n, tok, chan), bf16), ((n, tok, half), bf16)],
         (parts, n, n, n, n),
     )
     cols = cols.reshape(whole)
@@ -625,12 +656,14 @@
         functools.partial(reduce_kernel, n, 0),
         1,
         (mixed, term),
-        [(n, tok, half), whole],
-        (n, n, 1, 1),
+        [((tok, half), f32), (whole, bf16)],
+        (parts, parts, parts, parts, 1, 1),
+        [pltpu.VMEM((parts, tok, half), bf16)] * 3,
+        (0, 2),
     )
 
     def block_rows(rows, pieces):
-        return (rows + mask_own * jnp.sum(pieces.astype(f32), axis=0)).astype(bf16)
+        return (rows + mask_own * pieces).astype(bf16)
 
     start_rows = (signals.astype(f32) * mask_own).astype(bf16).astype(f32)
     handed = block_rows(start_rows, partial_rows)
@@ -638,7 +671,7 @@
         functools.partial(hand_kernel, n),
         2,
         (sliced(handed), handed),
-        [(n, tok, chan), (tok, half)],
+        [((n, tok, chan), bf16), ((tok, half), bf16)],
         (n + 1, n + 1, n),
     )
 
@@ -654,9 +687,9 @@
     back, back_cols = communicate(
         functools.partial(return_kernel, n),
         3,
-        (grads.reshape(2, total // 2, chan),),
-        [(parts, 2, total // 2, chan), (2, total // 2, chan)],
-        (n + 2, n + 2, n),
+        (grads.reshape(2, total // 2, chan).transpose(0, 2, 1),),
+        [((2, parts, chan, total // 2), bf16), ((2, chan, total // 2), bf16)],
+        (3, n + 2, n, parts),
     )
 
     def third_up():
@@ -665,11 +698,7 @@
         return convolve(taps_up).astype(bf16), jnp.zeros(whole, bf16), weight_slope(taps_up, slope)
 
     def third_down():
-        slope = local(
-            functools.partial(join_kernel, parts),
-            jax.ShapeDtypeStruct((total, half), bf16),
-            back.reshape(parts, total, chan),
-        )
+        slope = back.reshape(2, half, total // 2).transpose(0, 2, 1).reshape(total, half)
         return jnp.zeros((n, tok, half), bf16), convolve_back(slope), weight_slope(taps_down, slope)
 
     mixed, term, grad_weight = lax.cond(role_up, third_up, third_down)
@@ -677,12 +706,14 @@
         functools.partial(reduce_kernel, n, 1),
         4,
         (mixed, term),
-        [(n, tok, half), whole],
-        (n, n, 1, 1),
+        [((tok, half), f32), (whole, bf16)],
+        (parts, parts, parts, parts, 1, 1),
+        [pltpu.VMEM((parts, tok, half), bf16)] * 3,
+        (0, 2),
     )
 
     def last_down():
-        slope = input_slope(term, other, normed_down, scale_down, back_cols.reshape(whole))
+        slope = input_slope(term, other, normed_down, scale_down, back_cols.transpose(0, 2, 1).reshape(whole))
         return (mask * slope).astype(bf16)
 
     def last_up():
@@ -693,7 +724,7 @@
         functools.partial(collect_kernel, n),
         5,
         (grads.reshape(n, tok, chan),),
-        [(parts, tok, chan)],
+        [((parts, tok, chan), bf16)],
         (parts, parts),
     )
     down_rows = pieces.transpose(1, 0, 2).reshape(tok, half)

time: 187 us -> 170 us (0.909)
  the two profiles are of different devices: /device:TPU:14 before, /device:TPU:0 now
where the time goes in v1:
time: 170 us
  Pallas kernels  116 us (68%)
  local copies, waits for them, and re-layouts  25 us (15%)
  matrix products  17.5 us (10%)
  other arithmetic  9.99 us (6%)
    pallas_call x6, Pallas kernels, communicate(): pl.pallas_call(body, out_shape=[jax.ShapeDtypeStruct(shape, dtype) for sh...  113 us
    another operation x8, local copies, waits for them, and re-layouts  12.2 us
    conv_general_dilated x1, matrix products, convolve_back(): lax.conv_general_dilated(slope.reshape(samples, SIDE, SIDE, half), conv_w...  6.67 us
    dot_general x1, matrix products, convolve(): jnp.dot(taps, weight.reshape(9 * lanes, half), preferred_element_type=f32)  5.78 us
    dot_general x1, matrix products, weight_slope(): lax.dot_general(taps, slope.reshape(total, half), (((0,), (0,)), ((), ())...  5.05 us
    unnamed x15, local copies, waits for them, and re-layouts  3.6 us

profile of v1, /device:TPU:0, one launch (start us, length us, event | category | flops | bytes accessed | tf_op | source)
XLA Modules:
  0.0 169.6 jit_solution(2851425027717514501)
XLA Ops:
  0.6 1.0 fusion.43
  1.7 0.4 copy-done.8
  2.3 1.1 copy.80
  3.3 0.2 copy.81
  3.5 0.9 copy-done.1
  4.4 15.1 %shard_map.50 = (bf16[8,256,96]{2,1,0:T(8,128)(2,1)S(1)}, bf16[8,256,384]{2,1,0:T(8,128)(2,1)S(1)}) custom-call(bf16[256,384]{1,0:T(8,128)(2,1)S(1)} %copy-done.1, bf16[4,256,96]{2,1,0:T(8,128)(2,1)S(1)} %bitcast.140), custom_call_target="tpu_custom_call" | custom-call | tf_op jit(solution)/shard_map/pallas_call | solution.py:216
  19.5 0.4 fusion.40
  19.9 0.1 reshape.334
  20.0 0.1 reduce_sum.175
  20.1 0.1 reshape.335
  20.2 0.1 reduce_sum.179
  20.3 0.9 multiply_reduce_fusion.5
  21.4 0.1 sub.81
  21.5 0.1 broadcast_in_dim_reshape.4
  21.7 0.5 multiply_convert_fusion.3
  22.2 0.1 pad.14.active_ref
  22.3 2.8 %shard_map.51 = bf16[2048,1152]{1,0:T(8,128)(2,1)} custom-call(bf16[2048,128]{1,0:T(8,128)(2,1)S(1)} %pad.14.active_ref), custom_call_target="tpu_custom_call" | custom-call | tf_op jit(solution)/shard_map/pallas_call | solution.py:507
  25.3 8.0 %conditional.4 = (bf16[8,256,384]{2,1,0:T(8,128)(2,1)S(1)}, bf16[2,1024,96]{2,1,0:T(8,128)(2,1)S(1)}) conditional(s32[]{:T(128)} %convert_element_type.208, (bf16[96,9,384]{2,0,1:T(8,128)(2,1)S(1)}, bf16[2048,1152]{1,0:T(8,128)(2,1)}) %tuple.88, (bf16[8,256,384]{2,1,0:T(8,128)(2,1)S(1)}, f32[2,1024,1]{1,2,0:T(1,128)S(1)}, ...), branch_computations={%region_6.7_spmd, %region_7.8_spmd} | conditional | flops 1812725760 | bytes 26018240 | solution.py:654
  25.3 0.1 pad.10
  25.4 5.8 %fusion = bf16[2048,384]{0,1:T(8,128)(2,1)} fusion(bf16[1152,384]{1,0:T(8,128)(2,1)S(1)} %bitcast.164, bf16[2048,1152]{1,0:T(8,128)(2,1)} %get-tuple-element.72), kind=kOutput, calls=%fused_computation.1 | convolution fusion | flops 1812725760 | bytes 7176192 | tf_op jit(solution)/shard_map/cond/branch_0_fun/dot_general | solution.py:601
  31.1 1.9 %copy.95 = bf16[2048,384]{1,0:T(8,128)(2,1)S(1)} copy(bf16[2048,384]{0,1:T(8,128)(2,1)} %fusion) | data formatting | bytes 3145728 | tf_op jit(solution)/shard_map
  33.3 1.2 copy-done.6
  34.5 28.0 %shard_map.52 = (f32[256,384]{1,0:T(8,128)S(1)}, bf16[2,1024,96]{2,1,0:T(8,128)(2,1)}) custom-call(bf16[8,256,384]{2,1,0:T(8,128)(2,1)} %copy-done.6, bf16[2,1024,96]{2,1,0:T(8,128)(2,1)S(1)} %get-tuple-element.121.term_ref), custom_call_target="tpu_custom_call" | custom-call | tf_op jit(solution)/shard_map/pallas_call | solution.py:216
  62.6 0.1 add_convert_fusion.1.rows_ref
  62.8 0.1 copy.84
  62.9 0.2 copy.85
  63.1 16.9 %shard_map.53 = (bf16[8,256,96]{2,1,0:T(8,128)(2,1)S(1)}, bf16[256,384]{1,0:T(8,128)(2,1)S(1)}) custom-call(bf16[4,256,96]{2,1,0:T(8,128)(2,1)S(1)} %bitcast.139, bf16[256,384]{1,0:T(8,128)(2,1)S(1)} %add_convert_fusion.1.rows_ref), custom_call_target="tpu_custom_call" | custom-call | tf_op jit(solution)/shard_map/pallas_call | solution.py:216
  80.0 1.8 %conditional.5 = (bf16[2,1024,96]{2,1,0:T(8,128)(2,1)}, bf16[2,1024,96]{2,1,0:T(8,128)(2,1)}) conditional(s32[]{:T(128)} %convert_element_type.208, () %tuple.40, (f32[2,1024,1]{1,2,0:T(1,128)S(1)}, bf16[2,1024,96]{2,1,0:T(8,128)(2,1)S(1)}, bf16[8,256,96]{2,1,0:T(8,128)(2,1)S(1)}, f32[2]{0:T(128)S(1)}, bf16[2,1024,96]{2,1,0:T(8,128)(2,1)S(1)}, ...), branch_computations={%region_8.9_spmd, %region_9.20_spmd} | conditional | flops 7864896 | bytes 6799676 | solution.py:686
  80.0 0.9 broadcast.137
  80.9 0.9 broadcast.137.clone
  81.8 1.2 copy.86
  83.0 31.7 %shard_map.54 = (bf16[2,4,96,1024]{3,2,1,0:T(8,128)(2,1)}, bf16[2,96,1024]{2,1,0:T(8,128)(2,1)}) custom-call(bf16[2,96,1024]{2,1,0:T(8,128)(2,1)S(1)} %bitcast.137), custom_call_target="tpu_custom_call" | custom-call | tf_op jit(solution)/shard_map/pallas_call | solution.py:216
  114.7 26.0 %conditional.6 = (bf16[8,256,384]{2,1,0:T(8,128)(2,1)}, bf16[2,1024,96]{2,1,0:T(8,128)(2,1)S(1)}, f32[96,9,384]{2,0,1:T(8,128)}) conditional(s32[]{:T(128)} %convert_element_type.208, (bf16[2,4,96,1024]{3,2,1,0:T(8,128)(2,1)}, bf16[96,9,384]{2,0,1:T(8,128)(2,1)S(1)}, bf16[2048,1152]{1,0:T(8,128)(2,1)}) %tuple.90, (bf16[2,1024,96]{2,1,0:T(8,128)(2,1)}, ...), branch_computations={%region_20.21_spmd, %region_21.22_spmd} | conditional | flops 3174039552 | bytes 68419720 | solution.py:704
  115.0 1.9 %copy.73 = bf16[2,1024,384]{2,1,0:T(8,128)(2,1)S(1)} copy(bf16[2,1024,384]{1,2,0:T(8,128)(2,1)} %bitcast.161) | data formatting | bytes 3145728 | tf_op jit(solution)/shard_map/cond/branch_0_fun/transpose | solution.py:701
  116.8 0.6 copy.98
  117.4 0.2 pad.17.clone
  117.6 0.1 slice.22
  117.7 1.8 %fusion.17 = bf16[32,2,8,7,384]{4,0,3,2,1:T(8,128)(2,1)} fusion(bf16[32,2,7,2,384]{4,0,3,2,1:T(8,128)(2,1)S(1)} %slice.22, bf16[32,2,8,5,384]{4,0,3,2,1:T(8,128)(2,1)S(1)} %bitcast.144), kind=kLoop, calls=%fused_computation.18 | loop fusion | flops 8257536 | bytes 5406720 | tf_op jit(solution)/shard_map/cond/branch_0_fun/conv_general_dilated | solution.py:605
  119.5 0.9 rev.5
  120.5 6.7 %fusion.27 = bf16[32,16,5,96]{3,1,2,0:T(8,128)(2,1)S(1)} fusion(bf16[3,3,384,96]{2,3,1,0:T(8,128)(2,1)} %bitcast.169, bf16[32,2,8,7,384]{4,0,3,2,1:T(8,128)(2,1)} %fusion.17, pred[16,5]{0,1:T(8,128)(4,1)S(1)} %copy-done.11), kind=kOutput, calls=%fused_computation.24 | convolution fusion | flops 1663795200 | bytes 3907664 | tf_op jit(solution)/shard_map/cond/branch_0_fun/conv_general_dilated | solution.py:605
  127.1 0.2 copy.76
  127.4 0.2 copy.77
  127.6 6.8 %copy.87 = bf16[2048,1152]{0,1:T(8,128)(2,1)} copy(bf16[2048,1152]{1,0:T(8,128)(2,1)} %get-tuple-element.207) | data formatting | bytes 9437184 | tf_op jit(solution)/shard_map
  134.3 5.1 %fusion.21 = f32[96,9,384]{2,0,1:T(8,128)} fusion(bf16[2048,384,1]{1,0,2:T(8,128)(2,1)S(1)} %bitcast.153, bf16[9,128,2048]{2,1,0:T(8,128)(2,1)} %bitcast.156), kind=kOutput, calls=%fused_computation.22 | convolution fusion | flops 1358954496 | bytes 6438912 | tf_op jit(solution)/shard_map/cond/branch_0_fun/dot_general | solution.py:618
  139.4 1.3 broadcast.140
  140.7 9.4 %shard_map.55 = (f32[256,384]{1,0:T(8,128)S(1)}, bf16[2,1024,96]{2,1,0:T(8,128)(2,1)S(1)}) custom-call(bf16[8,256,384]{2,1,0:T(8,128)(2,1)} %get-tuple-element.129.mixed_ref, bf16[2,1024,96]{2,1,0:T(8,128)(2,1)S(1)} %get-tuple-element.130.term_ref), custom_call_target="tpu_custom_call" | custom-call | tf_op jit(solution)/shard_map/pallas_call | solution.py:216
  150.1 1.0 mul.309
  151.2 0.2 copy.89
  151.4 1.0 fusion.41
  152.4 4.1 %conditional.7 = (bf16[2,1024,96]{1,2,0:T(8,128)(2,1)S(1)}) conditional(s32[]{:T(128)} %convert_element_type.208, (f32[2,1024,1]{1,2,0:T(1,128)S(1)}, bf16[2,96,1024]{2,1,0:T(8,128)(2,1)}, f32[2,4]{1,0:T(2,128)S(1)}, f32[2,4,24]{2,1,0:T(4,128)S(1)}, bf16[2,1024,96]{2,1,0:T(8,128)(2,1)S(1)}, /*index=5*/bf16[2,1024,96]{2,1,0:T(8,128)(2,1)S(1)}, ...), branch_computations={%region_22.0_spmd, %region_27.28_spmd} | conditional | flops 7471496 | bytes 8700852 | solution.py:722
  152.4 0.2 copy.90
  152.6 0.2 copy.91
  152.9 2.0 %fusion.32 = (f32[2,96]{1,0:T(2,128)S(1)}, f32[2,96]{1,0:T(2,128)S(1)}, f32[2,1024,96]{1,2,0:T(8,128)S(1)}) fusion(bf16[2,1024,96]{1,2,0:T(8,128)(2,1)S(1)} %copy.91, bf16[2,1024,96]{1,2,0:T(8,128)(2,1)S(1)} %copy.90, f32[2,1024]{1,0:T(2,128)S(1)} %bitcast.170, f32[2,1024,96]{1,2,0:T(8,128)} %get-tuple-element.97, f32[2,1024,96]{1,2,0:T(8,128)} %get-tuple-element.95, ...), kind=kLoop, calls=%fused_computation.36 | loop fusion | flops 3341952 | bytes 3156224 | tf_op jit(solution)/shard_map/cond/branch_0_fun/reduce_sum | solution.py:577
  155.0 0.1 reduce_sum.143
  155.2 0.1 reduce_sum.148
  155.4 0.1 mul.262
  155.6 0.1 sub.72
  155.7 0.1 rsqrt.23
  155.8 0.6 fusion.31
  156.5 0.3 copy.92
  156.8 11.6 %shard_map.56 = bf16[4,256,96]{2,1,0:T(8,128)(2,1)S(1)} custom-call(bf16[8,256,96]{2,1,0:T(8,128)(2,1)S(1)} %bitcast.136), custom_call_target="tpu_custom_call" | custom-call | tf_op jit(solution)/shard_map/pallas_call | solution.py:216
  168.4 0.1 copy.93
  168.6 0.2 copy.94
  168.7 0.8 fusion.42
  (40 shorter events, 1.4 us)
Async XLA Ops:
  1.6 0.5 copy-start.8
  3.5 0.9 copy-start.1
  19.5 5.7 %copy-start.4 = (bf16[8,256,384]{2,1,0:T(8,128)(2,1)}, bf16[8,256,384]{2,1,0:T(8,128)(2,1)S(1)}, u32[]{:S(2)}) copy-start(bf16[8,256,384]{2,1,0:T(8,128)(2,1)S(1)} %get-tuple-element.119) | copy-start | bytes 4718596
  22.3 2.9 %copy-start.3 = (bf16[96,9,384]{2,0,1:T(8,128)(2,1)S(1)}, bf16[96,9,384]{2,0,1:T(8,128)(2,1)}, u32[]{:S(2)}) copy-start(bf16[96,9,384]{2,0,1:T(8,128)(2,1)} %param.12) | copy-start | bytes 1990660
  25.2 37.4 %copy-start.2 = (bf16[256,384]{1,0:T(8,128)(2,1)S(1)}, bf16[256,384]{1,0:T(8,128)(2,1)}, u32[]{:S(2)}) copy-start(bf16[256,384]{1,0:T(8,128)(2,1)} %rows_ref.1) | copy-start | bytes 589828
  33.3 1.2 copy-start.6
  33.3 46.7 %copy-start.9 = (s32[2]{0:T(128)S(1)}, s32[2]{0:T(128)}, u32[]{:S(2)}) copy-start(s32[2]{0:T(128)} %copy-done.8) | copy-start | bytes 28
  117.7 2.8 %copy-start.11 = (pred[16,5]{0,1:T(8,128)(4,1)S(1)}, pred[16,5]{0,1:T(8,128)(4,1)}, u32[]{:S(2)}) copy-start(pred[16,5]{0,1:T(8,128)(4,1)} %constant.88) | copy-start | bytes 244 | tf_op jit(solution)/shard_map/cond
  152.6 3.2 %copy-start.7 = (bf16[2,96,1024]{2,1,0:T(8,128)(2,1)S(1)}, bf16[2,96,1024]{2,1,0:T(8,128)(2,1)}, u32[]{:S(2)}) copy-start(bf16[2,96,1024]{2,1,0:T(8,128)(2,1)} %get-tuple-element.90) | copy-start | bytes 1179652 | tf_op jit(solution)/shard_map/cond

commit v2 on v1

--- a/solution.py
+++ b/solution.py
@@ -383,11 +383,13 @@
                     (2 + half, parts * half + j),
                 )
             )
-        copies.append(remote(rows_ref, own_ref, send.at[n], recv.at[n], (2 + half, f)))
         for copy in copies:
             copy.start()
         for copy in copies:
             copy.wait_send()
+        copy = remote(rows_ref, own_ref, send.at[n], recv.at[n], (2 + half, f))
+        copy.start()
+        copy.wait_send()
 
     @pl.when(jnp.logical_and(block == 1, half == f // parts))
     def _():
@@ -416,15 +418,16 @@
     @pl.when(block == 1)
     def _():
         greet([(0, f), (1, f)])
-        copies = [
-            remote(
-                grads_ref.at[half],
-                full_ref.at[half, f % parts],
-                send.at[0],
-                recv.at[2 * (f % parts) + half],
-                (f // parts, f),
-            )
-        ]
+        copy = remote(
+            grads_ref.at[half],
+            full_ref.at[half, f % parts],
+            send.at[0],
+            recv.at[2 * (f % parts) + half],
+            (f // parts, f),
+        )
+        copy.start()
+        copy.wait_send()
+        copies = []
         for core in range(2):
             copies.append(
                 remote(
@@ -503,17 +506,46 @@
             out_ref[base + area - SIDE : base + area, down] = edge
 
 
-def local(body, out, *args):
+def conv_kernel(samples, active_ref, weight_ref, out_ref, taps):
+    taps_kernel(samples, active_ref, taps)
+    step = 256
+
+    def chunk(i, carry):
+        rows = pl.ds(pl.multiple_of(i * step, step), step)
+        out_ref[rows, :] = jnp.dot(
+            taps[rows, :], weight_ref[...], preferred_element_type=jnp.float32
+        ).astype(out_ref.dtype)
+        return carry
+
+    lax.fori_loop(0, taps.shape[0] // step, chunk, 0)
+
+
+def local(body, out, scratch, *args):
     return pl.pallas_call(
         body,
         out_shape=out,
         in_specs=[pl.BlockSpec(memory_space=pltpu.VMEM)] * len(args),
         out_specs=pl.BlockSpec(memory_space=pltpu.VMEM),
+        scratch_shapes=scratch,
         compiler_params=pltpu.CompilerParams(vmem_limit_bytes=40 * 2**20),
     )(*args)
 
 
-def collect_kernel(n, grads_ref, out_ref, send, recv):
+def weight_slope(samples, active_ref, slope_ref, grad_ref, taps):
+    taps_kernel(samples, active_ref, taps)
+    step = 3 * active_ref.shape[1]
+
+    def chunk(i, carry):
+        rows = pl.ds(pl.multiple_of(i * step, step), step)
+        grad_ref[rows, :] = lax.dot_general(
+            taps[:, rows], slope_ref[...], (((0,), (0,)), ((), ())), preferred_element_type=jnp.float32
+        )
+        return carry
+
+    lax.fori_loop(0, 3, chunk, 0)
+
+
+def collect_kernel(n, samples, grads_ref, active_ref, slope_ref, out_ref, grad_ref, taps, send, recv):
     block, half, f = place()
     parts = n // 2
 
@@ -538,6 +570,10 @@
             def _():
                 pltpu.make_async_copy(grads_ref.at[piece], out_ref.at[mine], recv.at[mine]).start()
 
+    weight_slope(samples, active_ref, slope_ref, grad_ref, taps)
+
+    @pl.when(block == 0)
+    def _():
         for q0 in range(parts):
             piece = half * parts + (q0 + f) % parts
             own = jnp.logical_and((piece + n - 1) % n == f, half == f // parts)
@@ -588,17 +624,20 @@
 
     lanes = 128
 
-    def taps_of(active):
-        padded = jnp.pad(active.reshape(total, chan), ((0, 0), (0, lanes - chan)))
+    def padded(active):
+        return jnp.pad(active.reshape(total, chan), ((0, 0), (0, lanes - chan)))
+
+    wide = jnp.pad(conv_weight.transpose(1, 0, 2), ((0, 0), (0, lanes - chan), (0, 0))).reshape(9 * lanes, half)
+    taps_scratch = pltpu.VMEM((total, 9 * lanes), bf16)
+
+    def convolve(active):
         return local(
-            functools.partial(taps_kernel, samples),
-            jax.ShapeDtypeStruct((total, 9 * lanes), bf16),
-            padded,
-        )
-
-    def convolve(taps):
-        weight = jnp.pad(conv_weight.transpose(1, 0, 2), ((0, 0), (0, lanes - chan), (0, 0)))
-        return jnp.dot(taps, weight.reshape(9 * lanes, half), preferred_element_type=f32).reshape(n, tok, half)
+            functools.partial(conv_kernel, samples),
+            jax.ShapeDtypeStruct((total, half), bf16),
+            [taps_scratch],
+            active,
+            wide,
+        ).reshape(n, tok, half)
 
     def convolve_back(slope):
         return (
@@ -614,12 +653,6 @@
             .astype(bf16)
         )
 
-    def weight_slope(taps, slope):
-        whole_taps = lax.dot_general(
-            taps, slope.reshape(total, half), (((0,), (0,)), ((), ())), preferred_element_type=f32
-        )
-        return whole_taps.reshape(9, lanes, half)[:, :chan].transpose(1, 0, 2)
-
     def input_slope(term, other, normed, scale, grads):
         upstream = term.astype(f32) + other.astype(f32)
         gated = mask * upstream * silu_slope(normed)
@@ -642,10 +675,10 @@
 
     values = (cols.astype(f32) * mask).astype(bf16).astype(f32)
     normed_down, scale_down, active_down = normalize(values)
-    taps_down = taps_of(active_down)
+    active_down = padded(active_down)
 
     def first_down():
-        return convolve(taps_down).astype(bf16), jnp.zeros(whole, bf16)
+        return convolve(active_down), jnp.zeros(whole, bf16)
 
     def first_up():
         slope = (full.reshape(samples, area, half).astype(f32) * mask).astype(bf16)
@@ -678,12 +711,12 @@
     def second_up():
         normed, scale, active = normalize(skip_cols.reshape(whole).astype(f32))
         slope = mask * input_slope(term, other, normed, scale, cols)
-        return slope.astype(bf16), active
+        return slope.astype(bf16), padded(active)
 
     def second_down():
-        return jnp.zeros(whole, bf16), jnp.zeros(whole, bf16)
-
-    grads, active_up = lax.cond(role_up, second_up, second_down)
+        return jnp.zeros(whole, bf16), active_down
+
+    grads, active = lax.cond(role_up, second_up, second_down)
     back, back_cols = communicate(
         functools.partial(return_kernel, n),
         3,
@@ -694,14 +727,13 @@
 
     def third_up():
         slope = (full.reshape(samples, area, half).astype(f32) * mask).astype(bf16)
-        taps_up = taps_of(active_up)
-        return convolve(taps_up).astype(bf16), jnp.zeros(whole, bf16), weight_slope(taps_up, slope)
+        return convolve(active), jnp.zeros(whole, bf16), slope.reshape(total, half)
 
     def third_down():
         slope = back.reshape(2, half, total // 2).transpose(0, 2, 1).reshape(total, half)
-        return jnp.zeros((n, tok, half), bf16), convolve_back(slope), weight_slope(taps_down, slope)
-
-    mixed, term, grad_weight = lax.cond(role_up, third_up, third_down)
+        return jnp.zeros((n, tok, half), bf16), convolve_back(slope), slope
+
+    mixed, term, slope = lax.cond(role_up, third_up, third_down)
     partial_rows, other = communicate(
         functools.partial(reduce_kernel, n, 1),
         4,
@@ -720,13 +752,16 @@
         return jnp.zeros(whole, bf16)
 
     grads = lax.cond(role_up, last_up, last_down)
-    (pieces,) = communicate(
-        functools.partial(collect_kernel, n),
+    pieces, grad_weight = communicate(
+        functools.partial(collect_kernel, n, samples),
         5,
-        (grads.reshape(n, tok, chan),),
-        [((parts, tok, chan), bf16)],
+        (grads.reshape(n, tok, chan), active, slope),
+        [((parts, tok, chan), bf16), ((9 * lanes, half), f32)],
         (parts, parts),
-    )
+        [taps_scratch],
+        (1, 2, 4),
+    )
+    grad_weight = grad_weight.reshape(9, lanes, half)[:, :chan].transpose(1, 0, 2)
     down_rows = pieces.transpose(1, 0, 2).reshape(tok, half)
     results = jnp.where(role_up, block_rows(skip_rows.astype(f32), partial_rows), down_rows)
     return results, grad_weight

time: 170 us -> 170 us (level)
  matrix products: 17.5 us -> 6.68 us
  other arithmetic: 9.99 us -> 16.2 us
  Pallas kernels: 116 us -> 121 us
    dot_general x2 -> x0, matrix products: 10.8 us -> none  [the longest x1 5.78 us: convolve(): jnp.dot(taps, weight.reshape(9 * lanes, half), preferred_element_type=f32)]
    another operation x8 -> x6, local copies, waits for them, and re-layouts: 12.2 us -> 3.93 us
    pallas_call x1, Pallas kernels: 2.8 us -> 5.66 us  [local(): pl.pallas_call(body, out_shape=out, in_specs=[pl.BlockSpec(memory_space=p...]
    pallas_call x6, Pallas kernels: 113 us -> 116 us  [communicate(): pl.pallas_call(body, out_shape=[jax.ShapeDtypeStruct(shape, dtype) for sh...]
    pad x2 -> x3, local copies, waits for them, and re-layouts: 0.2 us -> 2.89 us  [the longest x2 1.86 us: padded(): return jnp.pad(active.reshape(total, chan), ((0, 0), (0, lanes - chan)))]
    convert_element_type x0 -> x2, local copies, waits for them, and re-layouts: none -> 2.38 us  [the longest x1 1.27 us: last_down(): return (mask * slope).astype(bf16)]
    convert_element_type x1, other arithmetic: 0.63 us -> 2.47 us  [last_down(): return (mask * slope).astype(bf16)]
    unnamed x15 -> x22, local copies, waits for them, and re-layouts: 3.6 us -> 4.74 us
where the time goes in v2:
time: 170 us
  Pallas kernels  121 us (71%)
  local copies, waits for them, and re-layouts  24.2 us (14%)
  other arithmetic  16.2 us (10%)
  matrix products  6.68 us (4%)
    pallas_call x6, Pallas kernels, communicate(): pl.pallas_call(body, out_shape=[jax.ShapeDtypeStruct(shape, dtype) for sh...  116 us
    conv_general_dilated x1, matrix products, convolve_back(): lax.conv_general_dilated(slope.reshape(samples, SIDE, SIDE, half), conv_w...  6.68 us
    pallas_call x1, Pallas kernels, local(): pl.pallas_call(body, out_shape=out, in_specs=[pl.BlockSpec(memory_space=p...  5.66 us
    unnamed x22, local copies, waits for them, and re-layouts  4.74 us
    another operation x6, local copies, waits for them, and re-layouts  3.93 us

profile of v2, /device:TPU:0, one launch (start us, length us, event | category | flops | bytes accessed | tf_op | source)
XLA Modules:
  0.0 169.5 jit_solution(2585372360451322490)
XLA Ops:
  0.6 1.0 fusion.32
  1.8 0.4 copy-done.9
  2.2 1.1 copy.125
  3.3 0.2 copy.126
  3.5 0.9 copy-done
  4.4 15.1 %shard_map.50 = (bf16[8,256,96]{2,1,0:T(8,128)(2,1)S(1)}, bf16[8,256,384]{2,1,0:T(8,128)(2,1)S(1)}) custom-call(bf16[256,384]{1,0:T(8,128)(2,1)S(1)} %copy-done, bf16[4,256,96]{2,1,0:T(8,128)(2,1)S(1)} %bitcast.121), custom_call_target="tpu_custom_call" | custom-call | tf_op jit(solution)/shard_map/pallas_call | solution.py:216
  19.5 0.4 fusion.29
  19.9 0.1 reduce_sum.175
  20.1 0.1 reduce_sum.179
  20.2 0.9 multiply_reduce_fusion.5
  21.3 0.1 sub.86
  21.6 0.1 copy.146
  21.7 0.3 mul.319.clone
  22.0 1.1 copy.148
  23.1 0.1 copy.128
  23.2 0.3 sub.87
  23.5 1.1 copy.147
  24.7 1.1 copy.127
  25.8 1.9 %multiply_convert_fusion.4 = bf16[2048,96]{0,1:T(8,128)(2,1)S(1)} fusion(f32[2048,96]{0,1:T(8,128)} %bitcast.142, f32[2048,96]{0,1:T(8,128)} %bitcast.143, f32[2048,96]{0,1:T(8,128)} %copy.127, f32[2048]{0:T(1024)S(1)} %reshape.361), kind=kLoop, calls=%fused_computation.56 | loop fusion | flops 2162688 | bytes 2760704 | tf_op jit(solution)/shard_map/convert_element_type | solution.py:623
  27.7 0.8 pad.12
  28.5 1.0 pad.13
  29.6 7.9 %conditional.4 = (bf16[8,256,384]{2,1,0:T(8,128)(2,1)S(1)}, bf16[2,1024,96]{2,1,0:T(8,128)(2,1)}) conditional(s32[]{:T(128)} %convert_element_type.201, (bf16[2048,128]{0,1:T(8,128)(2,1)}, bf16[1152,384]{1,0:T(8,128)(2,1)}) %tuple.40, (bf16[8,256,384]{2,1,0:T(8,128)(2,1)S(1)}, f32[2,1024,1]{1,2,0:T(1,128)S(1)}, ...), branch_computations={%region_6.7_spmd, %region_7.8_spmd} | conditional | flops 1674412032 | bytes 26018240 | solution.py:687
  29.7 1.4 copy.130.active_ref
  31.0 5.7 %branch_0_fun.1 = bf16[2048,384]{1,0:T(8,128)(2,1)S(1)} custom-call(bf16[2048,128]{1,0:T(8,128)(2,1)S(1)} %copy.130.active_ref, bf16[1152,384]{1,0:T(8,128)(2,1)} %get-tuple-element.72.weight_ref), custom_call_target="tpu_custom_call" | custom-call | tf_op jit(solution)/shard_map/cond/branch_0_fun/pallas_call | solution.py:524
  36.7 0.9 broadcast.138
  37.6 26.6 %shard_map.51 = (f32[256,384]{1,0:T(8,128)S(1)}, bf16[2,1024,96]{2,1,0:T(8,128)(2,1)}) custom-call(bf16[8,256,384]{2,1,0:T(8,128)(2,1)S(1)} %get-tuple-element.121.mixed_ref, bf16[2,1024,96]{2,1,0:T(8,128)(2,1)} %get-tuple-element.122.term_ref), custom_call_target="tpu_custom_call" | custom-call | tf_op jit(solution)/shard_map/pallas_call | solution.py:216
  64.3 0.1 add_convert_fusion.1.rows_ref
  64.5 0.1 copy.132
  64.6 0.2 copy.133
  64.8 19.5 %shard_map.52 = (bf16[8,256,96]{2,1,0:T(8,128)(2,1)S(1)}, bf16[256,384]{1,0:T(8,128)(2,1)S(1)}) custom-call(bf16[4,256,96]{2,1,0:T(8,128)(2,1)S(1)} %bitcast.120, bf16[256,384]{1,0:T(8,128)(2,1)S(1)} %add_convert_fusion.1.rows_ref), custom_call_target="tpu_custom_call" | custom-call | tf_op jit(solution)/shard_map/pallas_call | solution.py:216
  84.3 0.6 convert_multiply_fusion.3
  84.9 1.1 conditional.5
  84.9 1.0 copy.141
  86.0 0.2 copy.135
  86.2 34.7 %shard_map.53 = (bf16[2,4,96,1024]{3,2,1,0:T(8,128)(2,1)}, bf16[2,96,1024]{2,1,0:T(8,128)(2,1)}) custom-call(bf16[2,96,1024]{2,1,0:T(8,128)(2,1)S(1)} %bitcast.119), custom_call_target="tpu_custom_call" | custom-call | tf_op jit(solution)/shard_map/pallas_call | solution.py:216
  120.9 13.0 %conditional.6 = (bf16[8,256,384]{2,1,0:T(8,128)(2,1)S(1)}, bf16[2,1024,96]{2,1,0:T(8,128)(2,1)S(1)}, bf16[2048,384]{1,0:T(8,128)(2,1)S(1)}) conditional(s32[]{:T(128)} %convert_element_type.201, (bf16[2,4,96,1024]{3,2,1,0:T(8,128)(2,1)}, bf16[96,9,384]{2,0,1:T(8,128)(2,1)S(1)}) %tuple.89, (bf16[2048,128]{1,0:T(8,128)(2,1)}, ...), branch_computations={%region_20.21_spmd, %region_21.22_spmd} | conditional | flops 1672052736 | bytes 25977288 | solution.py:736
  120.9 1.9 %copy.118 = bf16[2,1024,384]{2,1,0:T(8,128)(2,1)S(1)} copy(bf16[2,1024,384]{1,2,0:T(8,128)(2,1)} %bitcast.147) | data formatting | bytes 3145728 | tf_op jit(solution)/shard_map/cond/branch_0_fun/transpose | solution.py:733
  122.8 0.6 copy.144
  123.3 0.2 pad.16.clone
  123.5 0.1 slice.18
  123.7 1.8 %fusion.14 = bf16[32,2,8,7,384]{4,0,3,2,1:T(8,128)(2,1)} fusion(bf16[32,2,7,2,384]{4,0,3,2,1:T(8,128)(2,1)S(1)} %slice.18, bf16[32,2,8,5,384]{4,0,3,2,1:T(8,128)(2,1)S(1)} %bitcast.129), kind=kLoop, calls=%fused_computation.14 | loop fusion | flops 8257536 | bytes 5406720 | tf_op jit(solution)/shard_map/cond/branch_0_fun/conv_general_dilated | solution.py:644
  125.5 0.9 rev.5
  126.4 6.7 %fusion.21 = bf16[32,16,5,96]{3,1,2,0:T(8,128)(2,1)S(1)} fusion(bf16[3,3,384,96]{2,3,1,0:T(8,128)(2,1)} %bitcast.152, bf16[32,2,8,7,384]{4,0,3,2,1:T(8,128)(2,1)} %fusion.14, pred[16,5]{0,1:T(8,128)(4,1)S(1)} %copy-done.12), kind=kOutput, calls=%fused_computation.19 | convolution fusion | flops 1663795200 | bytes 3907664 | tf_op jit(solution)/shard_map/cond/branch_0_fun/conv_general_dilated | solution.py:644
  133.1 0.2 copy.121
  133.3 0.2 copy.122
  133.5 0.1 broadcast.146
  133.9 7.9 %shard_map.54 = (f32[256,384]{1,0:T(8,128)S(1)}, bf16[2,1024,96]{2,1,0:T(8,128)(2,1)}) custom-call(bf16[8,256,384]{2,1,0:T(8,128)(2,1)S(1)} %get-tuple-element.130.mixed_ref, bf16[2,1024,96]{2,1,0:T(8,128)(2,1)S(1)} %get-tuple-element.131.term_ref), custom_call_target="tpu_custom_call" | custom-call | tf_op jit(solution)/shard_map/pallas_call | solution.py:216
  141.8 1.0 mul.319
  142.9 1.0 copy.136
  143.9 2.0 %fusion.30 = f32[2,1024,96]{1,2,0:T(8,128)} fusion(bf16[2,1024,96]{1,2,0:T(8,128)(2,1)} %copy.136, f32[2,1024]{1,0:T(2,128)S(1)} %reshape.365), kind=kLoop, calls=%fused_computation.58 | loop fusion | flops 786432 | bytes 1187840 | tf_op jit(solution)/shard_map/convert_element_type | solution.py:676
  145.8 9.6 %conditional.7 = (bf16[8,256,96]{2,1,0:T(8,128)(2,1)S(1)}) conditional(s32[]{:T(128)} %convert_element_type.201, (f32[2,1024,1]{1,2,0:T(1,128)S(1)}, bf16[2,96,1024]{2,1,0:T(8,128)(2,1)}, f32[2,4]{1,0:T(2,128)S(1)}, f32[2,4,24]{2,1,0:T(4,128)S(1)}, bf16[2,1024,96]{2,1,0:T(8,128)(2,1)S(1)}, /*index=5*/bf16[2,1024,96]{2,1,0:T(8,128)(2,1)}, ...), branch_computations={%region_22.0_spmd, %region_27.28_spmd} | conditional | flops 7471496 | bytes 9487284 | solution.py:754
  145.8 0.2 copy.137
  146.1 1.3 copy.138
  147.4 2.8 %fusion.27 = (f32[2,96]{1,0:T(2,128)S(1)}, f32[2,96]{1,0:T(2,128)S(1)}, f32[2,1024,96]{1,2,0:T(8,128)}) fusion(bf16[2,1024,96]{1,2,0:T(8,128)(2,1)S(1)} %copy.138, bf16[2,1024,96]{1,2,0:T(8,128)(2,1)S(1)} %copy.137, f32[2,1024]{1,0:T(2,128)S(1)} %bitcast.155, f32[2,1024,96]{1,2,0:T(8,128)} %get-tuple-element.96, f32[2,1024,96]{1,2,0:T(8,128)} %get-tuple-element.94, ...), kind=kLoop, calls=%fused_computation.33 | loop fusion | flops 3341952 | bytes 3156224 | tf_op jit(solution)/shard_map/cond/branch_0_fun/reduce_sum | solution.py:613
  150.2 0.1 reduce_sum.143
  150.4 0.1 reduce_sum.148
  150.5 0.7 broadcast_divide_fusion.1
  151.7 2.5 %fusion.26 = bf16[2,1024,96]{1,2,0:T(8,128)(2,1)} fusion(bf16[2,96,1024]{2,1,0:T(8,128)(2,1)S(1)} %copy-done.6, f32[2,1024,96]{1,2,0:T(8,128)} %get-tuple-element.236, f32[2,96]{1,0:T(2,128)S(1)} %mul.272, f32[2,96]{1,0:T(2,128)S(1)} %sub.77, f32[2,96]{1,0:T(2,128)S(1)} %rsqrt.23, f32[2,1024]{1,0:T(2,128)S(1)} %bitcast.156, ...), kind=kLoop, calls=%fused_computation.25 | loop fusion | flops 4128768 | bytes 2369792 | tf_op jit(solution)/shard_map/cond/branch_0_fun/convert_element_type | solution.py:749
  154.2 1.3 copy.124
  155.5 11.7 %shard_map.55 = (bf16[4,256,96]{2,1,0:T(8,128)(2,1)S(1)}, f32[1152,384]{1,0:T(8,128)S(1)}) custom-call(bf16[8,256,96]{2,1,0:T(8,128)(2,1)S(1)} %get-tuple-element.262.grads_ref, bf16[2048,128]{1,0:T(8,128)(2,1)} %get-tuple-element.129.active_ref, bf16[2048,384]{1,0:T(8,128)(2,1)S(1)} %get-tuple-element.135.slope_ref), custom_call_target="tpu_custom_call" | custom-call | tf_op jit(solution)/shard_map/pallas_call | solution.py:216
  167.2 1.2 slice_bitcast_fusion.2
  168.4 0.1 copy.139
  168.5 0.2 copy.140
  168.7 0.8 fusion.31
  (49 shorter events, 1.9 us)
Async XLA Ops:
  1.6 0.5 copy-start.9
  3.4 0.9 copy-start
  19.4 10.2 %copy-start.2 = (bf16[8,256,384]{2,1,0:T(8,128)(2,1)}, bf16[8,256,384]{2,1,0:T(8,128)(2,1)S(1)}, u32[]{:S(2)}) copy-start(bf16[8,256,384]{2,1,0:T(8,128)(2,1)S(1)} %get-tuple-element.120) | copy-start | bytes 4718596
  24.6 3.9 %copy-start.4 = (bf16[96,9,384]{2,0,1:T(8,128)(2,1)S(1)}, bf16[96,9,384]{2,0,1:T(8,128)(2,1)}, u32[]{:S(2)}) copy-start(bf16[96,9,384]{2,0,1:T(8,128)(2,1)} %param.12) | copy-start | bytes 1990660
  29.6 34.7 %copy-start.1 = (bf16[256,384]{1,0:T(8,128)(2,1)S(1)}, bf16[256,384]{1,0:T(8,128)(2,1)}, u32[]{:S(2)}) copy-start(bf16[256,384]{1,0:T(8,128)(2,1)} %rows_ref.1) | copy-start | bytes 589828
  37.6 46.7 %copy-start.10 = (s32[2]{0:T(128)S(1)}, s32[2]{0:T(128)}, u32[]{:S(2)}) copy-start(s32[2]{0:T(128)} %copy-done.9) | copy-start | bytes 28
  37.6 47.3 %copy-start.5 = (bf16[2048,128]{0,1:T(8,128)(2,1)S(1)}, bf16[2048,128]{0,1:T(8,128)(2,1)}, u32[]{:S(2)}) copy-start(bf16[2048,128]{0,1:T(8,128)(2,1)} %pad.12) | copy-start | bytes 1572868
  64.3 20.5 %copy-start.7 = (f32[256,1]{0,1:T(1,128)}, f32[256,1]{0,1:T(1,128)S(1)}, u32[]{:S(2)}) copy-start(f32[256,1]{0,1:T(1,128)S(1)} %constant_dynamic-slice_fusion) | copy-start | bytes 3076
  123.6 2.8 %copy-start.12 = (pred[16,5]{0,1:T(8,128)(4,1)S(1)}, pred[16,5]{0,1:T(8,128)(4,1)}, u32[]{:S(2)}) copy-start(pred[16,5]{0,1:T(8,128)(4,1)} %constant.85) | copy-start | bytes 244 | tf_op jit(solution)/shard_map/cond
  146.0 5.7 %copy-start.6 = (bf16[2,96,1024]{2,1,0:T(8,128)(2,1)S(1)}, bf16[2,96,1024]{2,1,0:T(8,128)(2,1)}, u32[]{:S(2)}) copy-start(bf16[2,96,1024]{2,1,0:T(8,128)(2,1)} %get-tuple-element.89) | copy-start | bytes 1179652 | tf_op jit(solution)/shard_map/cond
  155.5 13.2 %copy-start.8 = (f32[256,1]{0,1:T(1,128)S(1)}, f32[256,1]{0,1:T(1,128)}, u32[]{:S(2)}) copy-start(f32[256,1]{0,1:T(1,128)} %copy-done.7) | copy-start | bytes 3076

commit v3 on v2

--- a/solution.py
+++ b/solution.py
@@ -506,6 +506,10 @@
             out_ref[base + area - SIDE : base + area, down] = edge
 
 
+def copy_kernel(in_ref, out_ref):
+    out_ref[...] = in_ref[...]
+
+
 def conv_kernel(samples, active_ref, weight_ref, out_ref, taps):
     taps_kernel(samples, active_ref, taps)
     step = 256
@@ -625,7 +629,8 @@
     lanes = 128
 
     def padded(active):
-        return jnp.pad(active.reshape(total, chan), ((0, 0), (0, lanes - chan)))
+        out = jax.ShapeDtypeStruct((total, lanes), bf16)
+        return local(copy_kernel, out, [], jnp.pad(active.reshape(total, chan), ((0, 0), (0, lanes - chan))))
 
     wide = jnp.pad(conv_weight.transpose(1, 0, 2), ((0, 0), (0, lanes - chan), (0, 0))).reshape(9 * lanes, half)
     taps_scratch = pltpu.VMEM((total, 9 * lanes), bf16)

time: 170 us -> 165 us (0.971)
  local copies, waits for them, and re-layouts: 24.2 us -> 20.5 us
  other arithmetic: 16.2 us -> 13.9 us
    pad x2 -> x1, local copies, waits for them, and re-layouts: 1.86 us -> 0.11 us  [padded(): jnp.pad(active.reshape(total, chan), ((0, 0), (0, lanes - chan)))]
    unnamed x22 -> x39, local copies, waits for them, and re-layouts: 4.74 us -> 3.12 us
    another operation x6 -> x5, local copies, waits for them, and re-layouts: 3.93 us -> 4.31 us
    pallas_call x1 -> x2, Pallas kernels: 5.66 us -> 5.73 us  [local(): pl.pallas_call(body, out_shape=out, in_specs=[pl.BlockSpec(memory_space=p...]
where the time goes in v3:
time: 165 us; the launch traced here: 164 us
  Pallas kernels  122 us (74%)
  local copies, waits for them, and re-layouts  20.5 us (12%)
  other arithmetic  13.9 us (8%)
  matrix products  6.68 us (4%)
    pallas_call x6, Pallas kernels, communicate(): pl.pallas_call(body, out_shape=[jax.ShapeDtypeStruct(shape, dtype) for sh...  116 us
    conv_general_dilated x1, matrix products, convolve_back(): lax.conv_general_dilated(slope.reshape(samples, SIDE, SIDE, half), conv_w...  6.68 us
    pallas_call x2, Pallas kernels, local(): pl.pallas_call(body, out_shape=out, in_specs=[pl.BlockSpec(memory_space=p...  5.73 us
    another operation x5, local copies, waits for them, and re-layouts  4.31 us

profile of v3, /device:TPU:0, one launch (start us, length us, event | category | flops | bytes accessed | tf_op | source)
XLA Modules:
  0.0 163.9 jit_solution(18012348046073111295)
XLA Ops:
  0.6 1.0 fusion.33
  1.9 1.1 copy.115
  3.0 0.2 copy.116
  3.1 0.9 copy-done
  4.1 15.1 %shard_map.50 = (bf16[8,256,96]{2,1,0:T(8,128)(2,1)S(1)}, bf16[8,256,384]{2,1,0:T(8,128)(2,1)S(1)}) custom-call(bf16[256,384]{1,0:T(8,128)(2,1)S(1)} %copy-done, bf16[4,256,96]{2,1,0:T(8,128)(2,1)S(1)} %bitcast.129), custom_call_target="tpu_custom_call" | custom-call | tf_op jit(solution)/shard_map/pallas_call | solution.py:216
  19.2 0.4 fusion.30
  19.5 0.1 reshape.335
  19.6 0.1 reduce_sum.175
  19.7 0.1 reshape.336
  19.8 0.1 reduce_sum.179
  19.9 0.9 multiply_reduce_fusion.5
  21.0 0.1 sub.86
  21.2 0.1 broadcast_in_dim_reshape.4
  21.3 0.3 copy-done.12
  21.6 0.5 multiply_convert_fusion.2
  22.1 0.1 pad.11.in_ref
  22.2 1.0 pad.12
  23.3 0.1 reshape.364
  23.4 5.8 %conditional.4 = (bf16[8,256,384]{2,1,0:T(8,128)(2,1)S(1)}, bf16[2,1024,96]{2,1,0:T(8,128)(2,1)S(1)}) conditional(s32[]{:T(128)} %convert_element_type.201, (bf16[2048,128]{1,0:T(8,128)(2,1)S(1)}, bf16[1152,384]{1,0:T(8,128)(2,1)}) %tuple.40, (bf16[8,256,384]{2,1,0:T(8,128)(2,1)S(1)}, f32[2,1024,1]{1,2,0:T(1,128)S(1)}, ...), branch_computations={%region_6.7_spmd, %region_7.8_spmd} | conditional | flops 1674412032 | bytes 26018240 | solution.py:692
  23.4 5.7 %branch_0_fun.1 = bf16[2048,384]{1,0:T(8,128)(2,1)S(1)} custom-call(bf16[2048,128]{1,0:T(8,128)(2,1)S(1)} %get-tuple-element.71.active_ref, bf16[1152,384]{1,0:T(8,128)(2,1)} %get-tuple-element.72.weight_ref), custom_call_target="tpu_custom_call" | custom-call | tf_op jit(solution)/shard_map/cond/branch_0_fun/pallas_call | solution.py:528
  29.3 26.7 %shard_map.52 = (f32[256,384]{1,0:T(8,128)S(1)}, bf16[2,1024,96]{2,1,0:T(8,128)(2,1)}) custom-call(bf16[8,256,384]{2,1,0:T(8,128)(2,1)S(1)} %get-tuple-element.121.mixed_ref, bf16[2,1024,96]{2,1,0:T(8,128)(2,1)S(1)} %get-tuple-element.122.term_ref), custom_call_target="tpu_custom_call" | custom-call | tf_op jit(solution)/shard_map/pallas_call | solution.py:216
  56.0 0.1 reshape.360
  56.1 0.1 add_convert_fusion.1.rows_ref
  56.2 0.1 copy.119
  56.4 0.2 copy.120
  56.5 21.6 %shard_map.53 = (bf16[8,256,96]{2,1,0:T(8,128)(2,1)S(1)}, bf16[256,384]{1,0:T(8,128)(2,1)S(1)}) custom-call(bf16[4,256,96]{2,1,0:T(8,128)(2,1)S(1)} %bitcast.128, bf16[256,384]{1,0:T(8,128)(2,1)S(1)} %add_convert_fusion.1.rows_ref), custom_call_target="tpu_custom_call" | custom-call | tf_op jit(solution)/shard_map/pallas_call | solution.py:216
  78.2 0.9 conditional.5
  78.2 0.9 broadcast.140
  79.1 1.2 copy.122
  80.3 33.8 %shard_map.54 = (bf16[2,4,96,1024]{3,2,1,0:T(8,128)(2,1)}, bf16[2,96,1024]{2,1,0:T(8,128)(2,1)}) custom-call(bf16[2,96,1024]{2,1,0:T(8,128)(2,1)S(1)} %bitcast.127), custom_call_target="tpu_custom_call" | custom-call | tf_op jit(solution)/shard_map/pallas_call | solution.py:216
  114.2 12.8 %conditional.6 = (bf16[8,256,384]{2,1,0:T(8,128)(2,1)S(1)}, bf16[2,1024,96]{2,1,0:T(8,128)(2,1)S(1)}, bf16[2048,384]{1,0:T(8,128)(2,1)S(1)}) conditional(s32[]{:T(128)} %convert_element_type.201, (bf16[2,4,96,1024]{3,2,1,0:T(8,128)(2,1)}, bf16[96,9,384]{2,0,1:T(8,128)(2,1)S(1)}) %tuple.89, (bf16[2048,128]{1,0:T(8,128)(2,1)S(1)}, ...), branch_computations={%region_20.21_spmd, %region_21.22_spmd} | conditional | flops 1672052736 | bytes 25977288 | solution.py:741
  114.2 1.9 %copy.108 = bf16[2,1024,384]{2,1,0:T(8,128)(2,1)S(1)} copy(bf16[2,1024,384]{1,2,0:T(8,128)(2,1)} %bitcast.151) | data formatting | bytes 3145728 | tf_op jit(solution)/shard_map/cond/branch_0_fun/transpose | solution.py:738
  116.1 0.6 copy.129
  116.6 0.2 pad.15.clone
  116.8 0.1 slice.18
  116.9 1.8 %fusion.15 = bf16[32,2,8,7,384]{4,0,3,2,1:T(8,128)(2,1)} fusion(bf16[32,2,7,2,384]{4,0,3,2,1:T(8,128)(2,1)S(1)} %slice.18, bf16[32,2,8,5,384]{4,0,3,2,1:T(8,128)(2,1)S(1)} %bitcast.137), kind=kLoop, calls=%fused_computation.30 | loop fusion | flops 8257536 | bytes 5406720 | tf_op jit(solution)/shard_map/cond/branch_0_fun/conv_general_dilated | solution.py:649
  118.8 0.9 rev.5
  119.7 6.7 %fusion.22 = bf16[32,16,5,96]{3,1,2,0:T(8,128)(2,1)S(1)} fusion(bf16[3,3,384,96]{2,3,1,0:T(8,128)(2,1)} %bitcast.156, bf16[32,2,8,7,384]{4,0,3,2,1:T(8,128)(2,1)} %fusion.15, pred[16,5]{0,1:T(8,128)(4,1)S(1)} %copy-done.21), kind=kOutput, calls=%fused_computation.35 | convolution fusion | flops 1663795200 | bytes 3907664 | tf_op jit(solution)/shard_map/cond/branch_0_fun/conv_general_dilated | solution.py:649
  126.4 0.2 copy.111
  126.6 0.2 copy.112
  126.8 0.1 broadcast.146
  127.0 7.9 %shard_map.55 = (f32[256,384]{1,0:T(8,128)S(1)}, bf16[2,1024,96]{2,1,0:T(8,128)(2,1)}) custom-call(bf16[8,256,384]{2,1,0:T(8,128)(2,1)S(1)} %get-tuple-element.130.mixed_ref, bf16[2,1024,96]{2,1,0:T(8,128)(2,1)S(1)} %get-tuple-element.131.term_ref), custom_call_target="tpu_custom_call" | custom-call | tf_op jit(solution)/shard_map/pallas_call | solution.py:216
  135.0 1.0 mul.319
  136.0 0.1 reshape.365
  136.0 1.0 copy.123
  137.0 2.0 %fusion.31 = f32[2,1024,96]{1,2,0:T(8,128)} fusion(bf16[2,1024,96]{1,2,0:T(8,128)(2,1)} %copy.123, f32[2,1024]{1,0:T(2,128)S(1)} %reshape.365), kind=kLoop, calls=%fused_computation.61 | loop fusion | flops 786432 | bytes 1187840 | tf_op jit(solution)/shard_map/convert_element_type | solution.py:681
  139.0 11.0 %conditional.7 = (bf16[8,256,96]{2,1,0:T(8,128)(2,1)S(1)}) conditional(s32[]{:T(128)} %convert_element_type.201, (f32[2,1024,1]{1,2,0:T(1,128)S(1)}, bf16[2,96,1024]{2,1,0:T(8,128)(2,1)}, f32[2,4]{1,0:T(2,128)S(1)}, f32[2,4,24]{2,1,0:T(4,128)S(1)}, bf16[2,1024,96]{2,1,0:T(8,128)(2,1)}, /*index=5*/bf16[2,1024,96]{2,1,0:T(8,128)(2,1)}, ...), branch_computations={%region_22.0_spmd, %region_27.28_spmd} | conditional | flops 7471496 | bytes 7914392 | solution.py:759
  139.0 1.2 copy.124
  140.2 2.0 %copy.125 = bf16[2,1024,96]{1,2,0:T(8,128)(2,1)} copy(bf16[2,1024,96]{2,1,0:T(8,128)(2,1)} %get-tuple-element.246) | data formatting | bytes 786432 | tf_op jit(solution)/shard_map
  142.2 2.9 %fusion.28 = (f32[2,96]{1,0:T(2,128)S(1)}, f32[2,96]{1,0:T(2,128)S(1)}, f32[2,1024,96]{1,2,0:T(8,128)}) fusion(bf16[2,1024,96]{1,2,0:T(8,128)(2,1)} %copy.125, bf16[2,1024,96]{1,2,0:T(8,128)(2,1)S(1)} %copy.124, f32[2,1024]{1,0:T(2,128)S(1)} %bitcast.159, f32[2,1024,96]{1,2,0:T(8,128)} %get-tuple-element.96, f32[2,1024,96]{1,2,0:T(8,128)} %get-tuple-element.94, ...), kind=kLoop, calls=%fused_computation.49 | loop fusion | flops 3341952 | bytes 3156224 | tf_op jit(solution)/shard_map/cond/branch_0_fun/reduce_sum | solution.py:617
  145.1 0.1 reshape.322
  145.2 0.1 reduce_sum.143
  145.4 0.1 reduce_sum.148
  145.6 0.1 mul.272
  145.7 0.1 sub.77
  145.9 0.1 rsqrt.23
  146.0 2.7 %fusion.27 = bf16[2,1024,96]{1,2,0:T(8,128)(2,1)} fusion(bf16[2,96,1024]{2,1,0:T(8,128)(2,1)} %get-tuple-element.89, f32[2,1024,96]{1,2,0:T(8,128)} %get-tuple-element.261, f32[2,96]{1,0:T(2,128)S(1)} %mul.272, f32[2,96]{1,0:T(2,128)S(1)} %sub.77, f32[2,96]{1,0:T(2,128)S(1)} %rsqrt.23, f32[2,1024]{1,0:T(2,128)S(1)} %bitcast.160, ...), kind=kLoop, calls=%fused_computation.41 | loop fusion | flops 4128768 | bytes 2369792 | tf_op jit(solution)/shard_map/cond/branch_0_fun/convert_element_type | solution.py:754
  148.7 1.3 copy.114
  150.0 0.8 copy-done.7
  150.8 10.8 %shard_map.56 = (bf16[4,256,96]{2,1,0:T(8,128)(2,1)S(1)}, f32[1152,384]{1,0:T(8,128)S(1)}) custom-call(bf16[8,256,96]{2,1,0:T(8,128)(2,1)} %copy-done.7, bf16[2048,128]{1,0:T(8,128)(2,1)S(1)} %get-tuple-element.129.active_ref, bf16[2048,384]{1,0:T(8,128)(2,1)S(1)} %get-tuple-element.135.slope_ref), custom_call_target="tpu_custom_call" | custom-call | tf_op jit(solution)/shard_map/pallas_call | solution.py:216
  161.6 1.2 slice_bitcast_fusion.2
  162.7 0.1 copy.126
  162.9 0.2 copy.127
  163.1 0.8 fusion.32
  (59 shorter events, 1.2 us)
Async XLA Ops:
  0.6 21.6 %copy-start.4 = (bf16[96,9,384]{2,0,1:T(8,128)(2,1)S(1)}, bf16[96,9,384]{2,0,1:T(8,128)(2,1)}, u32[]{:S(2)}) copy-start(bf16[96,9,384]{2,0,1:T(8,128)(2,1)} %param.12) | copy-start | bytes 1990660
  1.6 1.3 copy-start.16
  1.6 1.3 copy-start.18
  3.1 0.9 copy-start
  19.1 4.3 %copy-start.2 = (bf16[8,256,384]{2,1,0:T(8,128)(2,1)}, bf16[8,256,384]{2,1,0:T(8,128)(2,1)S(1)}, u32[]{:S(2)}) copy-start(bf16[8,256,384]{2,1,0:T(8,128)(2,1)S(1)} %get-tuple-element.120) | copy-start | bytes 4718596
  20.9 0.6 copy-start.12
  21.1 2.3 %copy-start.10 = (f32[2,96]{1,0:T(2,128)}, f32[2,96]{1,0:T(2,128)S(1)}, u32[]{:S(2)}) copy-start(f32[2,96]{1,0:T(2,128)S(1)} %sub.86) | copy-start | bytes 2308
  21.2 2.2 %copy-start.8 = (f32[2,4,24]{2,1,0:T(4,128)}, f32[2,4,24]{2,1,0:T(4,128)S(1)}, u32[]{:S(2)}) copy-start(f32[2,4,24]{2,1,0:T(4,128)S(1)} %broadcast_in_dim.38) | copy-start | bytes 2308
  21.5 1.9 %copy-start.14 = (f32[2,96]{1,0:T(2,128)}, f32[2,96]{1,0:T(2,128)S(1)}, u32[]{:S(2)}) copy-start(f32[2,96]{1,0:T(2,128)S(1)} %add_rsqrt_fusion.2) | copy-start | bytes 2308
  23.4 32.7 %copy-start.1 = (bf16[256,384]{1,0:T(8,128)(2,1)S(1)}, bf16[256,384]{1,0:T(8,128)(2,1)}, u32[]{:S(2)}) copy-start(bf16[256,384]{1,0:T(8,128)(2,1)} %rows_ref.1) | copy-start | bytes 589828
  29.2 26.7 %copy-start.6 = (bf16[2,1024,96]{2,1,0:T(8,128)(2,1)}, bf16[2,1024,96]{2,1,0:T(8,128)(2,1)S(1)}, u32[]{:S(2)}) copy-start(bf16[2,1024,96]{2,1,0:T(8,128)(2,1)S(1)} %get-tuple-element.122.term_ref) | copy-start | bytes 1179652
  29.2 48.9 %copy-start.17 = (s32[2]{0:T(128)S(1)}, s32[2]{0:T(128)}, u32[]{:S(2)}) copy-start(s32[2]{0:T(128)} %copy-done.16) | copy-start | bytes 28
  29.2 48.9 %copy-start.19 = (s32[2]{0:T(128)S(1)}, s32[2]{0:T(128)}, u32[]{:S(2)}) copy-start(s32[2]{0:T(128)} %copy-done.18) | copy-start | bytes 28
  114.2 20.8 %copy-start.15 = (f32[2,96]{1,0:T(2,128)S(1)}, f32[2,96]{1,0:T(2,128)}, u32[]{:S(2)}) copy-start(f32[2,96]{1,0:T(2,128)} %copy-done.14) | copy-start | bytes 2308
  116.9 2.8 %copy-start.21 = (pred[16,5]{0,1:T(8,128)(4,1)S(1)}, pred[16,5]{0,1:T(8,128)(4,1)}, u32[]{:S(2)}) copy-start(pred[16,5]{0,1:T(8,128)(4,1)} %constant.85) | copy-start | bytes 244 | tf_op jit(solution)/shard_map/cond
  127.0 8.0 %copy-start.5 = (bf16[2,1024,96]{2,1,0:T(8,128)(2,1)}, bf16[2,1024,96]{2,1,0:T(8,128)(2,1)S(1)}, u32[]{:S(2)}) copy-start(bf16[2,1024,96]{2,1,0:T(8,128)(2,1)S(1)} %get-tuple-element.131.term_ref) | copy-start | bytes 1179652
  127.0 12.0 %copy-start.9 = (f32[2,4,24]{2,1,0:T(4,128)S(1)}, f32[2,4,24]{2,1,0:T(4,128)}, u32[]{:S(2)}) copy-start(f32[2,4,24]{2,1,0:T(4,128)} %copy-done.8) | copy-start | bytes 2308
  127.0 12.0 %copy-start.11 = (f32[2,96]{1,0:T(2,128)S(1)}, f32[2,96]{1,0:T(2,128)}, u32[]{:S(2)}) copy-start(f32[2,96]{1,0:T(2,128)} %copy-done.10) | copy-start | bytes 2308
  127.0 12.0 %copy-start.13 = (f32[2,4]{1,0:T(2,128)S(1)}, f32[2,4]{1,0:T(2,128)}, u32[]{:S(2)}) copy-start(f32[2,4]{1,0:T(2,128)} %copy-done.12) | copy-start | bytes 100
  150.0 0.8 copy-start.7
